TPU v7x, 512 devices: a whole 4x4x16 slice. The times are simulated.
512 devices in a mesh: sample: 16 (over y, z_hi), head: 32 (over z_lo, x, core).
Axes of the slice: x: 4, y: 4, z: 16 (z_hi: 4, z_lo: 4; z = z_hi * 4 + z_lo), core: 2. Of those that a mesh axis runs over, the one named last changes fastest.
Arguments:
- queries: bfloat16 [65536, 4096], P(('sample', 'head')), may hold values from -6 to 6
- keys: bfloat16 [65536, 1024], P(('sample', 'head')), may hold values from -6 to 6
- values: bfloat16 [65536, 1024], P(('sample', 'head')), may hold values from -6 to 6
- cotangent: bfloat16 [65536, 4096], P(('sample', 'head')), may hold values from -6 to 6
- prompt_keys: bfloat16 [8, 512, 128], P(None, 'sample'), may hold values from -6 to 6
- prompt_values: bfloat16 [8, 512, 128], P(None, 'sample'), may hold values from -6 to 6
- response_ids: int32 [16, 4096], P('sample'), may hold values from 0 to 31, never falling along the last dimension, each value on 1 to 256 neighbouring positions
- block_pattern: int32 [16, 32, 32], P('sample'), may hold values 0 or 1
Outputs:
- grad_queries: bfloat16 [65536, 4096], P(('sample', 'head'))
- grad_keys: bfloat16 [65536, 1024], P(('sample', 'head'))
- grad_values: bfloat16 [65536, 1024], P(('sample', 'head'))
Inputs may be any that keep to these rules, and one draw needn't show every extreme that they name: `response_ids`: along a group's 4096 positions the response number never falls; each response holds 1 to 256 positions and one holds exactly 256.
All inputs are finite; a program needn't handle non-finite values. No bound on the sum of `block_pattern` on one device may be relied on, other than what follows from the above.
Results may differ from a plain program's by a relative error of at most 0.022.
Values may be sent and summed in bfloat16 or wider, within the bound.
A program may use at most 64 MiB of HBM per device.

v0:
```python
import jax
import jax.numpy as jnp
from jax import lax
from jax.sharding import PartitionSpec as P

HEADS = 32
KVH = 8
MOST = 256
BLOCK = 128
QB = 512


def padded_tables(id_row, pattern, back):
    nblocks = pattern.shape[0]
    blocks = jnp.maximum(pattern, jnp.eye(nblocks, dtype=jnp.int32))
    blk_pad = jnp.concatenate([jnp.zeros((nblocks, back // BLOCK), jnp.int32), blocks], 1)
    id_pad = jnp.concatenate([jnp.full((back,), -1, jnp.int32), id_row])
    return (id_pad, blk_pad)


def window_mask(id_pad, blk_pad, back, start, rows_count, keys_count):
    row_ids = lax.dynamic_slice_in_dim(id_pad, start + back, rows_count)
    key_ids = lax.dynamic_slice_in_dim(id_pad, start, keys_count)
    rows = start + jnp.arange(rows_count, dtype=jnp.int32)
    places = start - back + jnp.arange(keys_count, dtype=jnp.int32)
    first = start // BLOCK
    sub = lax.dynamic_slice(blk_pad, (first, first), (rows_count // BLOCK, keys_count // BLOCK))
    spread = jnp.repeat(jnp.repeat(sub, BLOCK, 0), BLOCK, 1)
    return (
        (row_ids[:, None] == key_ids[None, :]) & (places[None, :] <= rows[:, None]) & (spread > 0)
    )


def tile_grads(query, upstream, first_keys, first_values, near_keys, near_values, allowed):
    scale = query.shape[-1] ** (-0.5)
    width = first_keys.shape[0]
    all_keys = jnp.concatenate([first_keys, near_keys], 0)
    all_values = jnp.concatenate([first_values, near_values], 0)
    scores = jnp.einsum("rgd,kd->grk", query, all_keys, preferred_element_type=jnp.float32) * scale
    visible = jnp.concatenate([jnp.ones((allowed.shape[0], width), jnp.bool_), allowed], 1)[None]
    scores = jnp.where(visible, scores, -1e30)
    peak = jnp.max(scores, -1, keepdims=True)
    expo = jnp.where(visible, jnp.exp(scores - peak), 0.0)
    weights = expo / jnp.sum(expo, -1, keepdims=True)
    dweights = jnp.einsum("rgd,kd->grk", upstream, all_values, preferred_element_type=jnp.float32)
    center = jnp.sum(weights * dweights, -1, keepdims=True)
    dscores = (weights * (dweights - center) * scale).astype(jnp.bfloat16)
    rounded = weights.astype(jnp.bfloat16)
    grad_query = jnp.einsum("grk,kd->rgd", dscores, all_keys, preferred_element_type=jnp.float32)
    grad_keys = jnp.einsum(
        "grk,rgd->kd", dscores[:, :, width:], query, preferred_element_type=jnp.float32
    )
    grad_values = jnp.einsum(
        "grk,rgd->kd", rounded[:, :, width:], upstream, preferred_element_type=jnp.float32
    )
    return (grad_query, grad_keys, grad_values)


def shards(
    queries, keys, values, cotangent, prompt_keys, prompt_values, response_ids, block_pattern
):
    tok_rows = queries.shape[0]
    head_dim = keys.shape[1] // KVH
    n_head = lax.axis_size("head")
    local = HEADS // n_head
    share = n_head // KVH
    moved = (
        lax.all_to_all(
            queries.reshape(tok_rows, n_head, local * head_dim),
            "head",
            split_axis=1,
            concat_axis=0,
            tiled=True,
        ),
        lax.all_to_all(
            cotangent.reshape(tok_rows, n_head, local * head_dim),
            "head",
            split_axis=1,
            concat_axis=0,
            tiled=True,
        ),
        lax.all_to_all(
            jnp.repeat(keys.reshape(tok_rows, KVH, head_dim), share, 1),
            "head",
            split_axis=1,
            concat_axis=0,
            tiled=True,
        ),
        lax.all_to_all(
            jnp.repeat(values.reshape(tok_rows, KVH, head_dim), share, 1),
            "head",
            split_axis=1,
            concat_axis=0,
            tiled=True,
        ),
    )
    head_q = moved[0]
    head_u = moved[1]
    group_rows = head_q.shape[0]
    key_pad = jnp.concatenate(
        [jnp.zeros((MOST, head_dim), jnp.bfloat16), moved[2].reshape(group_rows, head_dim)], 0
    )
    value_pad = jnp.concatenate(
        [jnp.zeros((MOST, head_dim), jnp.bfloat16), moved[3].reshape(group_rows, head_dim)], 0
    )
    kv_index = lax.axis_index("head") // share
    own_pk = lax.dynamic_index_in_dim(prompt_keys, kv_index, 0, keepdims=False)
    own_pv = lax.dynamic_index_in_dim(prompt_values, kv_index, 0, keepdims=False)
    first_k, first_v = (
        lax.all_gather(own_pk, "sample", axis=0, tiled=True),
        lax.all_gather(own_pv, "sample", axis=0, tiled=True),
    )
    id_pad, blk_pad = padded_tables(response_ids[0], block_pattern[0], MOST)

    def step(carry, index):
        acc_k, acc_v = carry
        start = index * QB
        block_q = lax.dynamic_slice_in_dim(head_q, start, QB)
        block_u = lax.dynamic_slice_in_dim(head_u, start, QB)
        near_k = lax.dynamic_slice_in_dim(key_pad, start, QB + MOST)
        near_v = lax.dynamic_slice_in_dim(value_pad, start, QB + MOST)
        allowed = window_mask(id_pad, blk_pad, MOST, start, QB, QB + MOST)
        grad_q, grad_k, grad_v = tile_grads(
            block_q, block_u, first_k, first_v, near_k, near_v, allowed
        )
        acc_k = lax.dynamic_update_slice_in_dim(
            acc_k, lax.dynamic_slice_in_dim(acc_k, start, QB + MOST) + grad_k, start, 0
        )
        acc_v = lax.dynamic_update_slice_in_dim(
            acc_v, lax.dynamic_slice_in_dim(acc_v, start, QB + MOST) + grad_v, start, 0
        )
        return ((acc_k, acc_v), grad_q.astype(jnp.bfloat16))

    empty = jnp.zeros((group_rows + MOST, head_dim), jnp.float32)
    (acc_k, acc_v), grad_blocks = lax.scan(
        step, (empty, empty), jnp.arange(group_rows // QB, dtype=jnp.int32)
    )
    grad_heads = grad_blocks.reshape(group_rows, 1, local * head_dim)
    grad_queries = lax.all_to_all(
        grad_heads, "head", split_axis=0, concat_axis=1, tiled=True
    ).reshape(tok_rows, HEADS * head_dim)
    back_k, back_v = (
        lax.all_to_all(
            acc_k[MOST:, None, :].astype(jnp.bfloat16),
            "head",
            split_axis=0,
            concat_axis=1,
            tiled=True,
        ).astype(jnp.float32),
        lax.all_to_all(
            acc_v[MOST:, None, :].astype(jnp.bfloat16),
            "head",
            split_axis=0,
            concat_axis=1,
            tiled=True,
        ).astype(jnp.float32),
    )
    grad_keys = (
        back_k.reshape(tok_rows, KVH, share, head_dim)
        .sum(2)
        .reshape(tok_rows, KVH * head_dim)
        .astype(jnp.bfloat16)
    )
    grad_values = (
        back_v.reshape(tok_rows, KVH, share, head_dim)
        .sum(2)
        .reshape(tok_rows, KVH * head_dim)
        .astype(jnp.bfloat16)
    )
    return (grad_queries, grad_keys, grad_values)


def solution(mesh):
    in_specs = (
        P(("sample", "head"), None),
        P(("sample", "head"), None),
        P(("sample", "head"), None),
        P(("sample", "head"), None),
        P(None, "sample", None),
        P(None, "sample", None),
        P("sample", None),
        P("sample", None, None),
    )
    out_specs = (
        P(("sample", "head"), None),
        P(("sample", "head"), None),
        P(("sample", "head"), None),
    )
    return jax.shard_map(shards, mesh=mesh, in_specs=in_specs, out_specs=out_specs, check_vma=False)
```

profile of v0, /device:TPU:7, one launch (start us, length us, event | category | flops | bytes accessed | tf_op | source)
XLA Modules:
  0.0 476.3 jit_solution(2417613510195050180)
XLA Ops:
  2.9 9.8 %all-to-all-start = ((bf16[128,32,128]{2,0,1:T(8,128)(2,1)}), bf16[128,32,128]{2,0,1:T(8,128)(2,1)S(1)}, u32[]{:S(2)}, u32[]{:S(2)}) async-start(bf16[128,32,128]{2,0,1:T(8,128)(2,1)} %bitcast.18), calls=%async_computation | async-start | bytes 2097152 | tf_op jit(solution)/shard_map/all_to_all | solution.py:82
  12.7 26.2 %all-to-all-done = bf16[128,32,128]{2,0,1:T(8,128)(2,1)S(1)} async-done(((bf16[128,32,128]{2,0,1:T(8,128)(2,1)}), bf16[128,32,128]{2,0,1:T(8,128)(2,1)S(1)}, u32[]{:S(2)}, u32[]{:S(2)}) %all-to-all-start) | async-done | bytes 1048608 | tf_op jit(solution)/shard_map/all_to_all | solution.py:82
  40.1 5.6 %all-to-all-start.2 = ((bf16[128,32,128]{2,0,1:T(8,128)(2,1)}), bf16[128,32,128]{2,0,1:T(8,128)(2,1)S(1)}, u32[]{:S(2)}, u32[]{:S(2)}) async-start(bf16[128,32,128]{2,0,1:T(8,128)(2,1)} %bitcast.27), calls=%async_computation.2 | async-start | bytes 2097152 | tf_op jit(solution)/shard_map/all_to_all | solution.py:89
  47.0 24.8 %all-to-all-done.2 = bf16[128,32,128]{2,0,1:T(8,128)(2,1)S(1)} async-done(((bf16[128,32,128]{2,0,1:T(8,128)(2,1)}), bf16[128,32,128]{2,0,1:T(8,128)(2,1)S(1)}, u32[]{:S(2)}, u32[]{:S(2)}) %all-to-all-start.2) | async-done | bytes 1048608 | tf_op jit(solution)/shard_map/all_to_all | solution.py:89
  71.8 5.7 %all-to-all-start.1 = ((bf16[128,32,128]{0,2,1:T(8,128)(2,1)}), bf16[128,32,128]{0,2,1:T(8,128)(2,1)S(1)}, u32[]{:S(2)}, u32[]{:S(2)}) async-start(bf16[128,32,128]{0,2,1:T(8,128)(2,1)} %bitcast.152), calls=%async_computation.1 | async-start | bytes 2097152 | tf_op jit(solution)/shard_map/all_to_all | solution.py:68
  77.5 2.3 copy.46
  79.8 23.9 %all-to-all-done.1 = bf16[128,32,128]{0,2,1:T(8,128)(2,1)S(1)} async-done(((bf16[128,32,128]{0,2,1:T(8,128)(2,1)}), bf16[128,32,128]{0,2,1:T(8,128)(2,1)S(1)}, u32[]{:S(2)}, u32[]{:S(2)}) %all-to-all-start.1) | async-done | bytes 1048608 | tf_op jit(solution)/shard_map/all_to_all | solution.py:68
  103.6 5.7 %all-to-all-start.3 = ((bf16[128,32,128]{0,2,1:T(8,128)(2,1)}), bf16[128,32,128]{0,2,1:T(8,128)(2,1)}, u32[]{:S(2)}, u32[]{:S(2)}) async-start(bf16[128,32,128]{0,2,1:T(8,128)(2,1)} %bitcast.151), calls=%async_computation.3 | async-start | bytes 2097152 | tf_op jit(solution)/shard_map/all_to_all | solution.py:75
  110.2 62.7 %all-gather = bf16[1,512,128]{2,1,0:T(8,128)(2,1)} all-gather(bf16[1,32,128]{2,1,0:T(8,128)(2,1)S(1)} %constant_dynamic-slice_fusion.3), channel_id=2, replica_groups=mesh['sample'=16,'head'=32] {'sample'}, dimensions={1}, use_global_device_ids=true | all-gather | bytes 139264 | tf_op jit(solution)/shard_map/all_gather | solution.py:110
  173.6 42.9 %all-gather.1 = bf16[1,512,128]{2,1,0:T(8,128)(2,1)} all-gather(bf16[1,32,128]{2,1,0:T(8,128)(2,1)S(1)} %constant_dynamic-slice_fusion.2), channel_id=3, replica_groups=mesh['sample'=16,'head'=32] {'sample'}, dimensions={1}, use_global_device_ids=true | all-gather | bytes 139264 | tf_op jit(solution)/shard_map/all_gather | solution.py:111
  220.0 2.3 copy.47
  222.4 1.5 broadcast_in_dim.61
  223.9 1.5 broadcast_in_dim.61.clone
  225.4 121.9 %while.16 = (s32[]{:T(128)}, f32[4352,128]{1,0:T(8,128)}, f32[4352,128]{1,0:T(8,128)}, bf16[8,512,1,128]{3,1,0,2:T(8,128)(2,1)}, s32[8]{0:T(128)S(1)}, /*index=5...) while((s32[]{:T(128)}, f32[4352,128]{1,0:T(8,128)}, ...), condition=%wide.region_4.5_spmd, body=%wide.region_0.4_spmd.sunk | while | flops 718274368 | bytes 30003508 | solution.py:135
  227.4 1.7 constant_dynamic-slice_fusion.5
  229.2 1.5 fusion.53
  231.7 1.7 multiply_reduce_fusion.2
  234.2 2.2 fusion.55
  238.4 2.2 fusion.56
  242.7 1.7 constant_dynamic-slice_fusion.5
  244.4 1.5 fusion.53
  246.9 1.7 multiply_reduce_fusion.2
  249.4 2.2 fusion.55
  253.7 2.2 fusion.56
  257.9 1.7 constant_dynamic-slice_fusion.5
  259.6 1.5 fusion.53
  262.2 1.7 multiply_reduce_fusion.2
  264.6 2.2 fusion.55
  268.9 2.2 fusion.56
  273.1 1.7 constant_dynamic-slice_fusion.5
  274.9 1.5 fusion.53
  277.4 1.7 multiply_reduce_fusion.2
  279.9 2.2 fusion.55
  284.1 2.2 fusion.56
  288.4 1.7 constant_dynamic-slice_fusion.5
  290.1 1.5 fusion.53
  292.6 1.8 multiply_reduce_fusion.2
  295.1 2.2 fusion.55
  299.4 2.2 fusion.56
  303.6 1.7 constant_dynamic-slice_fusion.5
  305.4 1.5 fusion.53
  307.9 1.7 multiply_reduce_fusion.2
  310.4 2.2 fusion.55
  314.7 2.2 fusion.56
  318.9 1.7 constant_dynamic-slice_fusion.5
  320.6 1.5 fusion.53
  323.1 1.7 multiply_reduce_fusion.2
  325.6 2.2 fusion.55
  329.9 2.2 fusion.56
  334.1 1.7 constant_dynamic-slice_fusion.5
  335.8 1.5 fusion.53
  338.4 1.7 multiply_reduce_fusion.2
  340.8 2.2 fusion.55
  345.1 2.2 fusion.56
  347.3 2.5 fusion.34
  352.9 26.0 %all-to-all-start.6 = ((bf16[32,2,8192]{2,1,0:T(2,128)(2,1)}), bf16[32,2,8192]{2,1,0:T(2,128)(2,1)S(1)}, u32[]{:S(2)}, u32[]{:S(2)}) async-start(bf16[32,2,8192]{2,1,0:T(2,128)(2,1)} %reshape.161), calls=%async_computation.6 | async-start | bytes 2097152 | tf_op jit(solution)/shard_map/all_to_all | solution.py:150
  379.0 1.4 reduce.15
  381.5 23.6 %all-to-all-done.6 = bf16[32,2,8192]{2,1,0:T(2,128)(2,1)S(1)} async-done(((bf16[32,2,8192]{2,1,0:T(2,128)(2,1)}), bf16[32,2,8192]{2,1,0:T(2,128)(2,1)S(1)}, u32[]{:S(2)}, u32[]{:S(2)}) %all-to-all-start.6) | async-done | bytes 1048608 | tf_op jit(solution)/shard_map/all_to_all | solution.py:150
  405.1 5.7 %all-to-all-start.5 = ((bf16[32,2,8192]{2,1,0:T(2,128)(2,1)}), bf16[32,2,8192]{2,1,0:T(2,128)(2,1)S(1)}, u32[]{:S(2)}, u32[]{:S(2)}) async-start(bf16[32,2,8192]{2,1,0:T(2,128)(2,1)} %reshape.159), calls=%async_computation.5 | async-start | bytes 2097152 | tf_op jit(solution)/shard_map/all_to_all | solution.py:143
  410.8 2.7 reduce.14
  414.6 22.4 %all-to-all-done.5 = bf16[32,2,8192]{2,1,0:T(2,128)(2,1)S(1)} async-done(((bf16[32,2,8192]{2,1,0:T(2,128)(2,1)}), bf16[32,2,8192]{2,1,0:T(2,128)(2,1)S(1)}, u32[]{:S(2)}, u32[]{:S(2)}) %all-to-all-start.5) | async-done | bytes 1048608 | tf_op jit(solution)/shard_map/all_to_all | solution.py:143
  437.9 5.7 %all-to-all-start.4 = ((bf16[32,2,8192]{2,1,0:T(2,128)(2,1)}), bf16[32,2,8192]{2,1,0:T(2,128)(2,1)}, u32[]{:S(2)}, u32[]{:S(2)}) async-start(bf16[32,2,8192]{2,1,0:T(2,128)(2,1)} %reshape.157), calls=%async_computation.4 | async-start | bytes 2097152 | tf_op jit(solution)/shard_map/all_to_all | solution.py:139
  450.7 19.1 %all-to-all-done.4 = bf16[32,2,8192]{2,1,0:T(2,128)(2,1)} async-done(((bf16[32,2,8192]{2,1,0:T(2,128)(2,1)}), bf16[32,2,8192]{2,1,0:T(2,128)(2,1)}, u32[]{:S(2)}, u32[]{:S(2)}) %all-to-all-start.4) | async-done | bytes 1048608 | tf_op jit(solution)/shard_map/all_to_all | solution.py:139
  469.9 4.3 reshape.158
  (193 shorter events, 66.1 us)
Async XLA Ops:
  0.6 1.0 copy-start
  0.6 12.0 %copy-start.5 = (bf16[128,1024]{1,0:T(8,128)(2,1)S(1)}, bf16[128,1024]{1,0:T(8,128)(2,1)}, u32[]{:S(2)}) copy-start(bf16[128,1024]{1,0:T(8,128)(2,1)} %param.12) | copy-start | bytes 786436
  2.9 36.0 %all-to-all-start = ((bf16[128,32,128]{2,0,1:T(8,128)(2,1)}), bf16[128,32,128]{2,0,1:T(8,128)(2,1)S(1)}, u32[]{:S(2)}, u32[]{:S(2)}) async-start(bf16[128,32,128]{2,0,1:T(8,128)(2,1)} %bitcast.18), calls=%async_computation | async-start | bytes 2097152 | tf_op jit(solution)/shard_map/all_to_all | solution.py:82
  12.7 33.0 %copy-start.4 = (bf16[128,4096]{1,0:T(8,128)(2,1)S(1)}, bf16[128,4096]{1,0:T(8,128)(2,1)}, u32[]{:S(2)}) copy-start(bf16[128,4096]{1,0:T(8,128)(2,1)} %param.10) | copy-start | bytes 3145732
  40.1 31.7 %all-to-all-start.2 = ((bf16[128,32,128]{2,0,1:T(8,128)(2,1)}), bf16[128,32,128]{2,0,1:T(8,128)(2,1)S(1)}, u32[]{:S(2)}, u32[]{:S(2)}) async-start(bf16[128,32,128]{2,0,1:T(8,128)(2,1)} %bitcast.27), calls=%async_computation.2 | async-start | bytes 2097152 | tf_op jit(solution)/shard_map/all_to_all | solution.py:89
  71.8 31.8 %all-to-all-start.1 = ((bf16[128,32,128]{0,2,1:T(8,128)(2,1)}), bf16[128,32,128]{0,2,1:T(8,128)(2,1)S(1)}, u32[]{:S(2)}, u32[]{:S(2)}) async-start(bf16[128,32,128]{0,2,1:T(8,128)(2,1)} %bitcast.152), calls=%async_computation.1 | async-start | bytes 2097152 | tf_op jit(solution)/shard_map/all_to_all | solution.py:68
  77.5 31.9 %copy-start.8 = (s32[1,32,32]{2,1,0:T(8,128)S(1)}, s32[1,32,32]{2,1,0:T(8,128)}, u32[]{:S(2)}) copy-start(s32[1,32,32]{2,1,0:T(8,128)} %param.17) | copy-start | bytes 12292
  77.5 32.0 %copy-start.7 = (s32[1,4096]{1,0:T(1,128)S(1)}, s32[1,4096]{1,0:T(1,128)}, u32[]{:S(2)}) copy-start(s32[1,4096]{1,0:T(1,128)} %param.16) | copy-start | bytes 49156
  103.6 116.4 %all-to-all-start.3 = ((bf16[128,32,128]{0,2,1:T(8,128)(2,1)}), bf16[128,32,128]{0,2,1:T(8,128)(2,1)}, u32[]{:S(2)}, u32[]{:S(2)}) async-start(bf16[128,32,128]{0,2,1:T(8,128)(2,1)} %bitcast.151), calls=%async_computation.3 | async-start | bytes 2097152 | tf_op jit(solution)/shard_map/all_to_all | solution.py:75
  230.7 0.9 copy-start.1
  230.7 1.0 copy-start.6
  245.9 0.9 copy-start.1
  245.9 1.0 copy-start.6
  261.1 0.9 copy-start.1
  261.2 1.0 copy-start.6
  276.4 0.9 copy-start.1
  276.4 1.0 copy-start.6
  291.6 0.9 copy-start.1
  291.6 1.0 copy-start.6
  306.9 0.9 copy-start.1
  306.9 1.0 copy-start.6
  322.1 0.9 copy-start.1
  322.1 1.0 copy-start.6
  337.4 0.9 copy-start.1
  337.4 1.0 copy-start.6
  352.9 52.2 %all-to-all-start.6 = ((bf16[32,2,8192]{2,1,0:T(2,128)(2,1)}), bf16[32,2,8192]{2,1,0:T(2,128)(2,1)S(1)}, u32[]{:S(2)}, u32[]{:S(2)}) async-start(bf16[32,2,8192]{2,1,0:T(2,128)(2,1)} %reshape.161), calls=%async_computation.6 | async-start | bytes 2097152 | tf_op jit(solution)/shard_map/all_to_all | solution.py:150
  405.1 31.8 %all-to-all-start.5 = ((bf16[32,2,8192]{2,1,0:T(2,128)(2,1)}), bf16[32,2,8192]{2,1,0:T(2,128)(2,1)S(1)}, u32[]{:S(2)}, u32[]{:S(2)}) async-start(bf16[32,2,8192]{2,1,0:T(2,128)(2,1)} %reshape.159), calls=%async_computation.5 | async-start | bytes 2097152 | tf_op jit(solution)/shard_map/all_to_all | solution.py:143
  436.9 1.0 copy-start.2
  437.9 31.9 %all-to-all-start.4 = ((bf16[32,2,8192]{2,1,0:T(2,128)(2,1)}), bf16[32,2,8192]{2,1,0:T(2,128)(2,1)}, u32[]{:S(2)}, u32[]{:S(2)}) async-start(bf16[32,2,8192]{2,1,0:T(2,128)(2,1)} %reshape.157), calls=%async_computation.4 | async-start | bytes 2097152 | tf_op jit(solution)/shard_map/all_to_all | solution.py:139
  444.7 3.6 copy-start.3
where the time goes:
time: 480 us; the launch traced here: 476 us
  waiting for transfers between devices  140 us (29%)
  blocking collectives  106 us (22%)
  matrix products  71.4 us (15%)
  local copies, waits for them, and re-layouts  65.8 us (14%)
  starting transfers between devices  64.1 us (13%)
  other arithmetic  22.5 us (5%)
  loops' own time  6 us (1%)
    all_gather x1, blocking collectives, shards(): lax.all_gather(own_pk, 'sample', axis=0, tiled=True)  62.7 us
    all_gather x1, blocking collectives, shards(): lax.all_gather(own_pv, 'sample', axis=0, tiled=True)  42.9 us
    all_to_all x1, waiting for transfers between devices, shards(): lax.all_to_all(jnp.repeat(keys.reshape(tok_rows, KVH, head_dim), share, 1...  26.2 us
    all_to_all x1, starting transfers between devices, shards(): lax.all_to_all(acc_v[MOST:, None, :].astype(jnp.bfloat16), 'head', split_...  26 us
    all_to_all x1, waiting for transfers between devices, shards(): lax.all_to_all(jnp.repeat(values.reshape(tok_rows, KVH, head_dim), share,...  24.8 us
    all_to_all x1, waiting for transfers between devices, shards(): lax.all_to_all(queries.reshape(tok_rows, n_head, local * head_dim), 'head...  23.9 us
    all_to_all x1, waiting for transfers between devices, shards(): lax.all_to_all(acc_v[MOST:, None, :].astype(jnp.bfloat16), 'head', split_...  23.6 us
    all_to_all x1, waiting for transfers between devices, shards(): lax.all_to_all(acc_k[MOST:, None, :].astype(jnp.bfloat16), 'head', split_...  22.4 us
  transfers between devices with their start and end apart: 7, of which 6 were waited for; matrix products, arithmetic and copies ran while one was open for 5% of the time, Pallas kernels for 0%

commit v1 on v0

v1 whole, which is shorter than its diff:
```python
import math

import jax
import jax.numpy as jnp
from jax import lax
from jax.experimental import pallas as pl
from jax.experimental.pallas import tpu as pltpu
from jax.sharding import PartitionSpec as P

KVH = 8
HD = 128
BLK = 128
SCALE = HD**-0.5
SCALE2 = SCALE * math.log2(math.e)
HIDE = -1e30
MESH = pl.DeviceIdType.MESH
BF = jnp.bfloat16
F32 = jnp.float32

NT = (((1,), (1,)), ((), ()))
NN = (((1,), (0,)), ((), ()))


def dot(a, b, dims):
    return lax.dot_general(a, b, dims, preferred_element_type=F32)


def tile_grads(q, u, pk, pv, kw, vw, bias, pk_t, kw_t):
    bias = jnp.concatenate([bias] * 4, 1)
    sp = dot(pk, q, NT) * SCALE2
    sw = dot(kw, q, NT) * SCALE2 + bias
    peak = jnp.maximum(jnp.max(sp, 0, keepdims=True), jnp.max(sw, 0, keepdims=True))
    ep = jnp.exp2(sp - peak)
    ew = jnp.exp2(sw - peak)
    inv = 1.0 / (jnp.sum(ep, 0, keepdims=True) + jnp.sum(ew, 0, keepdims=True))
    dp = dot(pv, u, NT)
    dw = dot(vw, u, NT)
    center = (jnp.sum(ep * dp, 0, keepdims=True) + jnp.sum(ew * dw, 0, keepdims=True)) * inv
    inv_s = inv * SCALE
    dsp = ((ep * inv_s) * (dp - center)).astype(BF)
    dsw = ((ew * inv_s) * (dw - center)).astype(BF)
    w = (ew * inv).astype(BF)
    gq = (dot(pk_t, dsp, NN) + dot(kw_t, dsw, NN)).T
    return gq, dot(dsw, q, NN), dot(w, u, NN)


def kernel(
    q_hbm, u_hbm, k_hbm, v_hbm, pk_hbm, pv_hbm, ids_hbm, pat_hbm,
    gq_hbm, gk_hbm, gv_hbm,
    ids, pat, bias, qb, ub, kw, vw, pkv, gs, gown, gnext, gqb, fin,
    sem_in, sem_small, sem_own,
    snd_a, rcv_a, snd_b, rcv_b, snd_c1, rcv_c1, snd_c2, rcv_c2,
    snd_sib, rcv_sib, snd_halo, rcv_halo, snd_gq, rcv_gq, sem_gq,
    snd_gsib, rcv_gsib, snd_gprev, rcv_gnext, sem_out,
):
    s = lax.axis_index("sample")
    hd = lax.axis_index("head")
    y, zh = s // 4, s % 4
    c, k = hd // 2, hd % 2
    zl = hd // 8
    first, last = c == 0, c == 15
    sib = (s, c * 2 + (1 - k))
    nxt = [(s, jnp.minimum(c + 1, 15) * 2 + i) for i in range(2)]
    prv = [(s, jnp.maximum(c - 1, 0) * 2 + i) for i in range(2)]
    zh_at = [lax.rem(zh + d, 4) for d in range(4)]
    zh_peer = [(y * 4 + zh_at[d], hd) for d in range(4)]
    zl_peer = [(s, lax.rem(hd + 8 * d, 32)) for d in range(4)]
    up, down, over = lax.rem(y + 1, 4), lax.rem(y + 3, 4), lax.rem(y + 2, 4)
    y_up, y_down = (up * 4 + zh, hd), (down * 4 + zh, hd)
    rows = pl.ds(pl.multiple_of(k * BLK, BLK), BLK)
    other = pl.ds(pl.multiple_of((1 - k) * BLK, BLK), BLK)
    own_rows = pl.ds(pl.multiple_of(256 + k * BLK, BLK), BLK)
    sib_rows = pl.ds(pl.multiple_of(256 + (1 - k) * BLK, BLK), BLK)

    def cols(core, h, width):
        return pl.ds(pl.multiple_of((core * 4 + h) * width, BLK), width)

    def send(src, dst, snd, rcv, where):
        return pltpu.make_async_remote_copy(
            src_ref=src, dst_ref=dst, send_sem=snd, recv_sem=rcv, device_id=where, device_id_type=MESH
        )

    barrier = pltpu.get_barrier_semaphore()

    def greet(where):
        pl.semaphore_signal(barrier, inc=1, device_id=where, device_id_type=MESH)

    for where in [sib] + zh_peer[1:] + zl_peer[1:] + [y_up, y_down]:
        greet(where)

    @pl.when(jnp.logical_not(last))
    def _():
        greet(nxt[0])
        greet(nxt[1])

    @pl.when(jnp.logical_not(first))
    def _():
        greet(prv[0])
        greet(prv[1])

    own_prompt = [
        pltpu.make_async_copy(src.at[pl.ds(k * 4, 4)], pkv.at[:, i, y, zh], sem_small.at[i])
        for i, src in enumerate((pk_hbm, pv_hbm))
    ]
    for copy in own_prompt:
        copy.start()
    small = [
        pltpu.make_async_copy(ids_hbm, ids, sem_small.at[2]),
        pltpu.make_async_copy(pat_hbm, pat, sem_small.at[3]),
    ]
    for copy in small:
        copy.start()

    def own_parts(h):
        return [
            pltpu.make_async_copy(q_hbm.at[:, cols(k, h, 512)], qb.at[h, rows], sem_in.at[h, 0]),
            pltpu.make_async_copy(u_hbm.at[:, cols(k, h, 512)], ub.at[h, rows], sem_in.at[h, 1]),
            pltpu.make_async_copy(k_hbm.at[:, cols(k, h, 128)], kw.at[h, own_rows], sem_in.at[h, 2]),
            pltpu.make_async_copy(v_hbm.at[:, cols(k, h, 128)], vw.at[h, own_rows], sem_in.at[h, 3]),
        ]

    for h in range(4):
        for copy in own_parts(h):
            copy.start()

    others = 9 + 2 * jnp.where(first, 0, 1) + 2 * jnp.where(last, 0, 1)
    pl.semaphore_wait(barrier, others)

    def part_a(d, i):
        src = (pk_hbm, pv_hbm)[i].at[k * 4 + zl]
        return send(src, pkv.at[zl, i, y, zh], snd_a.at[d, i], rcv_a.at[d, i], zh_peer[d])

    for d in (1, 3, 2):
        for i in range(2):
            part_a(d, i).start()

    def to_sib(h):
        far = 1 - k
        return [
            send(q_hbm.at[:, cols(far, h, 512)], qb.at[h, rows], snd_sib.at[h, 0], rcv_sib.at[h, 0], sib),
            send(u_hbm.at[:, cols(far, h, 512)], ub.at[h, rows], snd_sib.at[h, 1], rcv_sib.at[h, 1], sib),
            send(k_hbm.at[:, cols(far, h, 128)], kw.at[h, own_rows], snd_sib.at[h, 2], rcv_sib.at[h, 2], sib),
            send(v_hbm.at[:, cols(far, h, 128)], vw.at[h, own_rows], snd_sib.at[h, 3], rcv_sib.at[h, 3], sib),
        ]

    def halo(h, core, i):
        src, dst = ((k_hbm, kw), (v_hbm, vw))[i]
        return send(
            src.at[:, cols(core, h, 128)], dst.at[h, rows], snd_halo.at[h, core, i], rcv_halo.at[h, k, i], nxt[core]
        )

    for h in range(4):
        for copy in to_sib(h):
            copy.start()

        @pl.when(jnp.logical_not(last))
        def _(h=h):
            for core in range(2):
                for i in range(2):
                    halo(h, core, i).start()

    @pl.when(first)
    def _():
        kw[:, 0:256] = jnp.zeros((4, 256, HD), BF)
        vw[:, 0:256] = jnp.zeros((4, 256, HD), BF)

    @pl.when(last)
    def _():
        gnext[...] = jnp.zeros((8, 2, BLK, HD), BF)

    for copy in small:
        copy.wait()
    base = jnp.maximum(c - 1, 0) * 256
    id_rows = [
        ids[:, pl.ds(pl.multiple_of(base + b * BLK, BLK), BLK)].astype(F32) for b in range(2)
    ] + [ids[:, pl.ds(pl.multiple_of(c * 256 + b * BLK, BLK), BLK)].astype(F32) for b in range(2)]
    wide = [jnp.broadcast_to(r, (BLK, BLK)) for r in id_rows]
    tall = [w.T for w in wide]
    key_at = lax.broadcasted_iota(jnp.int32, (BLK, BLK), 0)
    row_at = lax.broadcasted_iota(jnp.int32, (BLK, BLK), 1)
    inside = jnp.where(first, 0, 1)
    for rb in range(2):
        at = 2 * c + rb
        for t in range(3):
            b = rb + t
            seen = tall[b] == wide[2 + rb]
            if t == 2:
                seen = seen & (key_at <= row_at)
            else:
                flag = pat[0, at, jnp.maximum(at - 2 + t, 0)]
                if b < 2:
                    flag = flag * inside
                seen = seen & (jnp.full((BLK, BLK), flag, jnp.int32) > 0)
            bias[rb, t * BLK : (t + 1) * BLK] = jnp.where(seen, 0.0, HIDE)

    def part_b(d, e):
        part = pkv.at[zl, :, y, zh_at[e]]
        return send(part, part, snd_b.at[d, e], rcv_b.at[zl, e], zl_peer[d])

    for copy in own_prompt:
        copy.wait()
    for e in (3, 1, 2):
        for i in range(2):
            part_a(4 - e, i).wait_recv()
        for d in (1, 3, 2):
            part_b(d, e).start()

    def part_c1(h, to):
        part = pkv.at[h, :, y]
        return send(part, part, snd_c1.at[h, to], rcv_c1.at[h, to], (y_up, y_down)[to])

    def c1_of(h, to, at):
        part = pkv.at[h, :, at]
        return send(part, part, snd_c1.at[h, to], rcv_c1.at[h, to], (y_up, y_down)[to])

    for h in range(4):

        @pl.when(zl != h)
        def _(h=h):
            for e in (3, 1, 2):
                part = pkv.at[h, :, y, zh_at[e]]
                send(part, part, snd_b.at[1, e], rcv_b.at[h, e], zl_peer[1]).wait_recv()

        for to in range(2):
            part_c1(h, to).start()

    def part_c2(h, to, at):
        part = pkv.at[h, to, at]
        return send(part, part, snd_c2.at[h, to], rcv_c2.at[h, to], (y_up, y_down)[to])

    def relay(h):
        c1_of(h, 0, down).wait_recv()
        part_c2(h, 0, down).start()
        c1_of(h, 1, up).wait_recv()
        part_c2(h, 1, up).start()

    def to_prev(h, core):
        part = gs.at[h, :, core * BLK : (core + 1) * BLK]
        return send(part, gnext.at[k * 4 + h], snd_gprev.at[h, core], rcv_gnext.at[k * 4 + h], prv[core])

    def grads_to_sib(h):
        return send(gs.at[h, :, sib_rows], gown.at[k * 4 + h], snd_gsib.at[h], rcv_gsib.at[h], sib)

    def gq_own(h):
        return pltpu.make_async_copy(gqb.at[h, rows], gq_hbm.at[:, cols(k, h, 512)], sem_gq.at[h])

    def gq_to_sib(h):
        return send(gqb.at[h, other], gq_hbm.at[:, cols(k, h, 512)], snd_gq.at[h], rcv_gq.at[h], sib)

    relay(0)

    @pl.loop(0, 4)
    def _(h):
        @pl.when(h < 3)
        def _():
            relay(h + 1)

        for copy in own_parts(h):
            copy.wait()
        for copy in to_sib(h):
            copy.wait_recv()
        for to in range(2):
            part_c2(h, to, over).wait_recv()

        @pl.when(jnp.logical_not(first))
        def _():
            for core in range(2):
                for i in range(2):
                    dst = (kw, vw)[i].at[h, core * BLK : (core + 1) * BLK]
                    send(dst, dst, snd_halo.at[h, core, i], rcv_halo.at[h, core, i], prv[0]).wait_recv()

        pk = pkv[h, 0].reshape(512, HD)
        pv = pkv[h, 1].reshape(512, HD)
        pk_t = pk.T
        kw_t = kw[h].T
        parts = []
        for rb in range(2):
            qr = qb[h, rb * BLK : (rb + 1) * BLK]
            ur = ub[h, rb * BLK : (rb + 1) * BLK]
            q = jnp.concatenate([qr[:, g * HD : (g + 1) * HD] for g in range(4)], 0)
            u = jnp.concatenate([ur[:, g * HD : (g + 1) * HD] for g in range(4)], 0)
            near = slice(rb * BLK, rb * BLK + 384)
            gq, gk, gv = tile_grads(q, u, pk, pv, kw[h, near], vw[h, near], bias[rb], pk_t, kw_t[:, near])
            for g in range(4):
                gqb[h, rb * BLK : (rb + 1) * BLK, g * HD : (g + 1) * HD] = gq[g * BLK : (g + 1) * BLK].astype(BF)
            parts.append((gk, gv))
        for i in range(2):
            a, b = parts[0][i], parts[1][i]
            gs[h, i, 0:128] = a[0:128].astype(BF)
            gs[h, i, 128:384] = (a[128:384] + b[0:256]).astype(BF)
            gs[h, i, 384:512] = b[256:384].astype(BF)

        @pl.when(jnp.logical_not(first))
        def _():
            for core in range(2):
                to_prev(h, core).start()

        grads_to_sib(h).start()
        gq_to_sib(h).start()
        gq_own(h).start()
        gown[k * 4 + h] = gs[h, :, own_rows]

    def outs(hh):
        return [
            pltpu.make_async_copy(fin.at[hh, i], out.at[:, hh * HD : (hh + 1) * HD], sem_out.at[hh, i])
            for i, out in enumerate((gk_hbm, gv_hbm))
        ]

    for h in range(4):
        send(gs.at[h, :, sib_rows], gown.at[(1 - k) * 4 + h], snd_gsib.at[h], rcv_gsib.at[h], sib).wait_recv()
        for core in range(2):

            @pl.when(jnp.logical_not(last))
            def _(core=core, h=h):
                part = gnext.at[core * 4 + h]
                send(part, part, snd_gprev.at[h, core], rcv_gnext.at[core * 4 + h], nxt[0]).wait_recv()

            hh = core * 4 + h
            fin[hh] = (gown[hh].astype(F32) + gnext[hh].astype(F32)).astype(BF)
            for copy in outs(hh):
                copy.start()

    for h in range(4):
        gq_own(h).wait()
        copy = gq_to_sib(h)
        copy.wait_send()
        send(gqb.at[h, rows], gq_hbm.at[:, cols(1 - k, h, 512)], snd_gq.at[h], rcv_gq.at[h], sib).wait_recv()
        grads_to_sib(h).wait_send()
        for copy in to_sib(h):
            copy.wait_send()
        for to in range(2):
            part_c1(h, to).wait_send()
        part_c2(h, 0, down).wait_send()
        part_c2(h, 1, up).wait_send()

    for d in (1, 2, 3):
        for i in range(2):
            part_a(d, i).wait_send()
        for e in (1, 2, 3):
            part_b(d, e).wait_send()

    @pl.when(jnp.logical_not(last))
    def _():
        for h in range(4):
            for core in range(2):
                for i in range(2):
                    halo(h, core, i).wait_send()

    @pl.when(jnp.logical_not(first))
    def _():
        for h in range(4):
            for core in range(2):
                to_prev(h, core).wait_send()

    for hh in range(KVH):
        for copy in outs(hh):
            copy.wait()


def shards(queries, keys, values, cotangent, prompt_keys, prompt_values, response_ids, block_pattern):
    anywhere = pl.BlockSpec(memory_space=pl.ANY)
    dma = pltpu.SemaphoreType.DMA
    return pl.pallas_call(
        kernel,
        out_shape=[
            jax.ShapeDtypeStruct(queries.shape, BF),
            jax.ShapeDtypeStruct(keys.shape, BF),
            jax.ShapeDtypeStruct(values.shape, BF),
        ],
        in_specs=[anywhere] * 8,
        out_specs=[anywhere] * 3,
        scratch_shapes=[
            pltpu.VMEM((1, 4096), jnp.int32),
            pltpu.SMEM((1, 32, 32), jnp.int32),
            pltpu.VMEM((2, 384, BLK), F32),
            pltpu.VMEM((4, 256, 512), BF),
            pltpu.VMEM((4, 256, 512), BF),
            pltpu.VMEM((4, 512, HD), BF),
            pltpu.VMEM((4, 512, HD), BF),
            pltpu.VMEM((4, 2, 4, 4, 32, HD), BF),
            pltpu.VMEM((4, 2, 512, HD), BF),
            pltpu.VMEM((8, 2, BLK, HD), BF),
            pltpu.VMEM((8, 2, BLK, HD), BF),
            pltpu.VMEM((4, 256, 512), BF),
            pltpu.VMEM((8, 2, BLK, HD), BF),
            dma((4, 4)), dma((4,)), dma((1,)),
            dma((4, 2)), dma((4, 2)), dma((4, 4)), dma((4, 4)), dma((4, 2)), dma((4, 2)), dma((4, 2)), dma((4, 2)),
            dma((4, 4)), dma((4, 4)), dma((4, 2, 2)), dma((4, 2, 2)), dma((4,)), dma((4,)), dma((4,)),
            dma((4,)), dma((4,)), dma((4, 2)), dma((8,)), dma((8, 2)),
        ],
        compiler_params=pltpu.CompilerParams(
            collective_id=0, has_side_effects=True, vmem_limit_bytes=48 << 20
        ),
        cost_estimate=pl.CostEstimate(flops=4 << 30, bytes_accessed=8 << 20, transcendentals=4 << 20),
        name="tree_attention_backward",
    )(queries, cotangent, keys, values, prompt_keys, prompt_values, response_ids, block_pattern)


def solution(mesh):
    tokens = P(("sample", "head"), None)
    prompt = P(None, "sample", None)
    return jax.shard_map(
        shards,
        mesh=mesh,
        in_specs=(tokens, tokens, tokens, tokens, prompt, prompt, P("sample", None), P("sample", None, None)),
        out_specs=(tokens, tokens, tokens),
        check_vma=False,
    )
```

time: 480 us -> 72.1 us (0.15)
  the two profiles are of different devices: /device:TPU:7 before, /device:TPU:69 now
where the time goes in v1:
time: 72.1 us; the launch traced here: 71.6 us
  Pallas kernels  61.1 us (85%)
  local copies, waits for them, and re-layouts  9.83 us (14%)
    pallas_call x1, Pallas kernels, shards(): pl.pallas_call(kernel, out_shape=[jax.ShapeDtypeStruct(queries.shape, BF)...  61.1 us
    unnamed x19, local copies, waits for them, and re-layouts  9.83 us

profile of v1, /device:TPU:69, one launch (start us, length us, event | category | flops | bytes accessed | tf_op | source)
XLA Modules:
  0.0 71.6 jit_solution(12332930628457003373)
XLA Ops:
  0.6 0.0 copy-start
  0.6 1.2 %copy-done = bf16[128,4096]{1,0:T(8,128)(2,1)S(1)} copy-done((bf16[128,4096]{1,0:T(8,128)(2,1)S(1)}, bf16[128,4096]{1,0:T(8,128)(2,1)}, u32[]{:S(2)}) %copy-start) | copy-done | bytes 1048600
  1.9 0.0 copy-start.1
  1.9 1.2 %copy-done.1 = bf16[128,4096]{1,0:T(8,128)(2,1)S(1)} copy-done((bf16[128,4096]{1,0:T(8,128)(2,1)S(1)}, bf16[128,4096]{1,0:T(8,128)(2,1)}, u32[]{:S(2)}) %copy-start.1) | copy-done | bytes 1048600
  3.1 0.0 copy-start.2
  3.1 0.9 %copy-done.2 = bf16[128,1024]{1,0:T(8,128)(2,1)S(1)} copy-done((bf16[128,1024]{1,0:T(8,128)(2,1)S(1)}, bf16[128,1024]{1,0:T(8,128)(2,1)}, u32[]{:S(2)}) %copy-start.2) | copy-done | bytes 262168
  4.0 0.0 copy-start.3
  4.0 0.9 %copy-done.3 = bf16[128,1024]{1,0:T(8,128)(2,1)S(1)} copy-done((bf16[128,1024]{1,0:T(8,128)(2,1)S(1)}, bf16[128,1024]{1,0:T(8,128)(2,1)}, u32[]{:S(2)}) %copy-start.3) | copy-done | bytes 262168
  5.0 0.0 copy-start.4
  5.0 0.8 %copy-done.4 = bf16[8,32,128]{2,1,0:T(8,128)(2,1)S(1)} copy-done((bf16[8,32,128]{2,1,0:T(8,128)(2,1)S(1)}, bf16[8,32,128]{2,1,0:T(8,128)(2,1)}, u32[]{:S(2)}) %copy-start.4) | copy-done | bytes 65560
  5.8 0.0 copy-start.5
  5.8 0.8 %copy-done.5 = bf16[8,32,128]{2,1,0:T(8,128)(2,1)S(1)} copy-done((bf16[8,32,128]{2,1,0:T(8,128)(2,1)S(1)}, bf16[8,32,128]{2,1,0:T(8,128)(2,1)}, u32[]{:S(2)}) %copy-start.5) | copy-done | bytes 65560
  6.7 0.0 copy-start.6
  6.7 0.7 copy-done.6
  7.4 0.0 copy-start.7
  7.4 0.7 copy-done.7
  8.1 61.1 %tree_attention_backward.1 = (bf16[128,4096]{1,0:T(8,128)(2,1)S(1)}, bf16[128,1024]{1,0:T(8,128)(2,1)S(1)}, bf16[128,1024]{1,0:T(8,128)(2,1)S(1)}) custom-call(bf16[128,4096]{1,0:T(8,128)(2,1)S(1)} %copy-done, bf16[128,4096]{1,0:T(8,128)(2,1)S(1)} %copy-done.1, bf16[128,1024]{1,0:T(8,128)(2,1)S(1)} %copy-done.2, bf16[128,1024]{1,0:T(8,128)(2,1)S(1)} %copy-done.3, ...), custom_call_target="tpu_custom_call" | custom-call | flops 4294967296 | bytes 8388608 | tf_op jit(solution)/shard_map/tree_attention_backward/pallas_call | solution.py:363
  69.3 1.0 %copy.14 = bf16[128,4096]{1,0:T(8,128)(2,1)} copy(bf16[128,4096]{1,0:T(8,128)(2,1)S(1)} %get-tuple-element.6) | data formatting | bytes 2097152
  70.2 0.7 copy.15
  70.9 0.7 copy.16
Async XLA Ops:
  0.6 1.2 %copy-start = (bf16[128,4096]{1,0:T(8,128)(2,1)S(1)}, bf16[128,4096]{1,0:T(8,128)(2,1)}, u32[]{:S(2)}) copy-start(bf16[128,4096]{1,0:T(8,128)(2,1)} %q_hbm.1) | copy-start | bytes 3145732
  1.9 1.2 %copy-start.1 = (bf16[128,4096]{1,0:T(8,128)(2,1)S(1)}, bf16[128,4096]{1,0:T(8,128)(2,1)}, u32[]{:S(2)}) copy-start(bf16[128,4096]{1,0:T(8,128)(2,1)} %u_hbm.1) | copy-start | bytes 3145732
  3.1 0.9 %copy-start.2 = (bf16[128,1024]{1,0:T(8,128)(2,1)S(1)}, bf16[128,1024]{1,0:T(8,128)(2,1)}, u32[]{:S(2)}) copy-start(bf16[128,1024]{1,0:T(8,128)(2,1)} %k_hbm.1) | copy-start | bytes 786436
  4.0 0.9 %copy-start.3 = (bf16[128,1024]{1,0:T(8,128)(2,1)S(1)}, bf16[128,1024]{1,0:T(8,128)(2,1)}, u32[]{:S(2)}) copy-start(bf16[128,1024]{1,0:T(8,128)(2,1)} %v_hbm.1) | copy-start | bytes 786436
  5.0 0.8 %copy-start.4 = (bf16[8,32,128]{2,1,0:T(8,128)(2,1)S(1)}, bf16[8,32,128]{2,1,0:T(8,128)(2,1)}, u32[]{:S(2)}) copy-start(bf16[8,32,128]{2,1,0:T(8,128)(2,1)} %pk_hbm.1) | copy-start | bytes 196612
  5.8 0.8 %copy-start.5 = (bf16[8,32,128]{2,1,0:T(8,128)(2,1)S(1)}, bf16[8,32,128]{2,1,0:T(8,128)(2,1)}, u32[]{:S(2)}) copy-start(bf16[8,32,128]{2,1,0:T(8,128)(2,1)} %pv_hbm.1) | copy-start | bytes 196612
  6.7 0.7 %copy-start.6 = (s32[1,4096]{1,0:T(1,128)S(1)}, s32[1,4096]{1,0:T(1,128)}, u32[]{:S(2)}) copy-start(s32[1,4096]{1,0:T(1,128)} %ids_hbm.1) | copy-start | bytes 49156
  7.4 0.7 %copy-start.7 = (s32[1,32,32]{2,1,0:T(8,128)S(1)}, s32[1,32,32]{2,1,0:T(8,128)}, u32[]{:S(2)}) copy-start(s32[1,32,32]{2,1,0:T(8,128)} %pat_hbm.1) | copy-start | bytes 12292

commit v2 on v1

--- a/solution.py
+++ b/solution.py
@@ -47,9 +47,9 @@
 def kernel(
     q_hbm, u_hbm, k_hbm, v_hbm, pk_hbm, pv_hbm, ids_hbm, pat_hbm,
     gq_hbm, gk_hbm, gv_hbm,
-    ids, pat, bias, qb, ub, kw, vw, pkv, gs, gown, gnext, gqb, fin,
+    ids, pat, bias, qb, ub, kw, vw, pkv, gs, gown, gnext, gqb, fin, acc,
     sem_in, sem_small, sem_own,
-    snd_a, rcv_a, snd_b, rcv_b, snd_c1, rcv_c1, snd_c2, rcv_c2,
+    snd_own, rcv_own, snd_z, rcv_z, snd_c, rcv_c,
     snd_sib, rcv_sib, snd_halo, rcv_halo, snd_gq, rcv_gq, sem_gq,
     snd_gsib, rcv_gsib, snd_gprev, rcv_gnext, sem_out,
 ):
@@ -57,16 +57,17 @@
     hd = lax.axis_index("head")
     y, zh = s // 4, s % 4
     c, k = hd // 2, hd % 2
-    zl = hd // 8
+    zl, x = hd // 8, c % 4
     first, last = c == 0, c == 15
     sib = (s, c * 2 + (1 - k))
     nxt = [(s, jnp.minimum(c + 1, 15) * 2 + i) for i in range(2)]
     prv = [(s, jnp.maximum(c - 1, 0) * 2 + i) for i in range(2)]
-    zh_at = [lax.rem(zh + d, 4) for d in range(4)]
-    zh_peer = [(y * 4 + zh_at[d], hd) for d in range(4)]
-    zl_peer = [(s, lax.rem(hd + 8 * d, 32)) for d in range(4)]
-    up, down, over = lax.rem(y + 1, 4), lax.rem(y + 3, 4), lax.rem(y + 2, 4)
-    y_up, y_down = (up * 4 + zh, hd), (down * 4 + zh, hd)
+    column = lax.rem(hd, 8)
+
+    def along_z(d, to_zl):
+        return (y * 4 + lax.rem(zh + d, 4), to_zl * 8 + column)
+
+    y_peer = [(lax.rem(y + d, 4) * 4 + zh, hd) for d in range(4)]
     rows = pl.ds(pl.multiple_of(k * BLK, BLK), BLK)
     other = pl.ds(pl.multiple_of((1 - k) * BLK, BLK), BLK)
     own_rows = pl.ds(pl.multiple_of(256 + k * BLK, BLK), BLK)
@@ -85,7 +86,10 @@
     def greet(where):
         pl.semaphore_signal(barrier, inc=1, device_id=where, device_id_type=MESH)
 
-    for where in [sib] + zh_peer[1:] + zl_peer[1:] + [y_up, y_down]:
+    upwards = [(2, 2, 1), (2, 2, 0), (3, 1, 3), (3, 1, 2), (3, 1, 1), (3, 1, 0)]
+    downwards = [(2, 2, 2), (2, 2, 3), (1, 3, 0), (1, 3, 1), (1, 3, 2), (1, 3, 3)]
+    source = {1: along_z(1, 0), 2: along_z(2, jnp.where(zl < 2, 3, 0)), 3: along_z(3, 3)}
+    for where in [sib] + y_peer[1:] + list(source.values()):
         greet(where)
 
     @pl.when(jnp.logical_not(last))
@@ -99,7 +103,7 @@
         greet(prv[1])
 
     own_prompt = [
-        pltpu.make_async_copy(src.at[pl.ds(k * 4, 4)], pkv.at[:, i, y, zh], sem_small.at[i])
+        pltpu.make_async_copy(src.at[pl.ds(k * 4, 4)], pkv.at[:, i, 0, 0], sem_small.at[i])
         for i, src in enumerate((pk_hbm, pv_hbm))
     ]
     for copy in own_prompt:
@@ -123,16 +127,36 @@
         for copy in own_parts(h):
             copy.start()
 
-    others = 9 + 2 * jnp.where(first, 0, 1) + 2 * jnp.where(last, 0, 1)
+    others = 4 + 6 * jnp.where((zl == 0) | (zl == 3), 1, 0) + 2 * jnp.where(first, 0, 1) + 2 * jnp.where(last, 0, 1)
     pl.semaphore_wait(barrier, others)
 
-    def part_a(d, i):
-        src = (pk_hbm, pv_hbm)[i].at[k * 4 + zl]
-        return send(src, pkv.at[zl, i, y, zh], snd_a.at[d, i], rcv_a.at[d, i], zh_peer[d])
-
-    for d in (1, 3, 2):
-        for i in range(2):
-            part_a(d, i).start()
+    def part_own(d):
+        return send(pkv.at[:, :, 0, 0], pkv.at[:, :, 4 - d, 0], snd_own.at[d], rcv_own.at[d], y_peer[d])
+
+    def part_z(h, j, slot, where):
+        return send(pkv.at[h, :, 0, 0], pkv.at[h, :, 0, slot], snd_z.at[h, j], rcv_z.at[h, slot], where)
+
+    def parts_z(h, way):
+        return [part_z(h, j, slot, along_z(d, to_zl)) for j, (slot, d, to_zl) in enumerate(way)]
+
+    def part_c(h, d):
+        src, dst = pkv.at[h, :, 0, 1:4], pkv.at[h, :, 4 - d, 1:4]
+        return send(src, dst, snd_c.at[h, d], rcv_c.at[h, d], y_peer[d])
+
+    turn = (2, 1, 3)
+
+    for copy in own_prompt:
+        copy.wait()
+    for at, way in ((3, upwards), (0, downwards)):
+
+        @pl.when(zl == at)
+        def _(way=way):
+            for h in range(4):
+                for copy in parts_z(h, way):
+                    copy.start()
+
+    for d in turn:
+        part_own(d).start()
 
     def to_sib(h):
         far = 1 - k
@@ -153,11 +177,13 @@
         for copy in to_sib(h):
             copy.start()
 
-        @pl.when(jnp.logical_not(last))
-        def _(h=h):
+    def halos():
+        for h in range(4):
             for core in range(2):
                 for i in range(2):
                     halo(h, core, i).start()
+
+    pl.when(x < 3)(halos)
 
     @pl.when(first)
     def _():
@@ -193,46 +219,17 @@
                 seen = seen & (jnp.full((BLK, BLK), flag, jnp.int32) > 0)
             bias[rb, t * BLK : (t + 1) * BLK] = jnp.where(seen, 0.0, HIDE)
 
-    def part_b(d, e):
-        part = pkv.at[zl, :, y, zh_at[e]]
-        return send(part, part, snd_b.at[d, e], rcv_b.at[zl, e], zl_peer[d])
-
-    for copy in own_prompt:
-        copy.wait()
-    for e in (3, 1, 2):
-        for i in range(2):
-            part_a(4 - e, i).wait_recv()
-        for d in (1, 3, 2):
-            part_b(d, e).start()
-
-    def part_c1(h, to):
-        part = pkv.at[h, :, y]
-        return send(part, part, snd_c1.at[h, to], rcv_c1.at[h, to], (y_up, y_down)[to])
-
-    def c1_of(h, to, at):
-        part = pkv.at[h, :, at]
-        return send(part, part, snd_c1.at[h, to], rcv_c1.at[h, to], (y_up, y_down)[to])
-
-    for h in range(4):
-
-        @pl.when(zl != h)
-        def _(h=h):
-            for e in (3, 1, 2):
-                part = pkv.at[h, :, y, zh_at[e]]
-                send(part, part, snd_b.at[1, e], rcv_b.at[h, e], zl_peer[1]).wait_recv()
-
-        for to in range(2):
-            part_c1(h, to).start()
-
-    def part_c2(h, to, at):
-        part = pkv.at[h, to, at]
-        return send(part, part, snd_c2.at[h, to], rcv_c2.at[h, to], (y_up, y_down)[to])
-
-    def relay(h):
-        c1_of(h, 0, down).wait_recv()
-        part_c2(h, 0, down).start()
-        c1_of(h, 1, up).wait_recv()
-        part_c2(h, 1, up).start()
+    def along_y(h):
+        for slot in (1, 3, 2):
+            part_z(h, 0, slot, source[slot]).wait_recv()
+        for d in turn:
+            part_c(h, d).start()
+
+    along_y(0)
+    pl.when((x == 3) & jnp.logical_not(last))(halos)
+    along_y(1)
+    for d in turn:
+        part_own(d).wait_recv()
 
     def to_prev(h, core):
         part = gs.at[h, :, core * BLK : (core + 1) * BLK]
@@ -247,20 +244,18 @@
     def gq_to_sib(h):
         return send(gqb.at[h, other], gq_hbm.at[:, cols(k, h, 512)], snd_gq.at[h], rcv_gq.at[h], sib)
 
-    relay(0)
-
     @pl.loop(0, 4)
     def _(h):
-        @pl.when(h < 3)
+        @pl.when(h < 2)
         def _():
-            relay(h + 1)
+            along_y(h + 2)
 
         for copy in own_parts(h):
             copy.wait()
         for copy in to_sib(h):
             copy.wait_recv()
-        for to in range(2):
-            part_c2(h, to, over).wait_recv()
+        for d in turn:
+            part_c(h, d).wait_recv()
 
         @pl.when(jnp.logical_not(first))
         def _():
@@ -273,8 +268,8 @@
         pv = pkv[h, 1].reshape(512, HD)
         pk_t = pk.T
         kw_t = kw[h].T
-        parts = []
-        for rb in range(2):
+
+        def half(rb):
             qr = qb[h, rb * BLK : (rb + 1) * BLK]
             ur = ub[h, rb * BLK : (rb + 1) * BLK]
             q = jnp.concatenate([qr[:, g * HD : (g + 1) * HD] for g in range(4)], 0)
@@ -283,17 +278,18 @@
             gq, gk, gv = tile_grads(q, u, pk, pv, kw[h, near], vw[h, near], bias[rb], pk_t, kw_t[:, near])
             for g in range(4):
                 gqb[h, rb * BLK : (rb + 1) * BLK, g * HD : (g + 1) * HD] = gq[g * BLK : (g + 1) * BLK].astype(BF)
-            parts.append((gk, gv))
+            return gk, gv
+
+        a = half(0)
         for i in range(2):
-            a, b = parts[0][i], parts[1][i]
-            gs[h, i, 0:128] = a[0:128].astype(BF)
-            gs[h, i, 128:384] = (a[128:384] + b[0:256]).astype(BF)
-            gs[h, i, 384:512] = b[256:384].astype(BF)
-
-        @pl.when(jnp.logical_not(first))
-        def _():
-            for core in range(2):
-                to_prev(h, core).start()
+            gs[h, i, 0:128] = a[i][0:128].astype(BF)
+            acc[i] = a[i][128:384]
+        pl.when(jnp.logical_not(first))(to_prev(h, 0).start)
+        b = half(1)
+        for i in range(2):
+            gs[h, i, 128:384] = (acc[i] + b[i][0:256]).astype(BF)
+            gs[h, i, 384:512] = b[i][256:384].astype(BF)
+        pl.when(jnp.logical_not(first))(to_prev(h, 1).start)
 
         grads_to_sib(h).start()
         gq_to_sib(h).start()
@@ -328,16 +324,18 @@
         grads_to_sib(h).wait_send()
         for copy in to_sib(h):
             copy.wait_send()
-        for to in range(2):
-            part_c1(h, to).wait_send()
-        part_c2(h, 0, down).wait_send()
-        part_c2(h, 1, up).wait_send()
-
-    for d in (1, 2, 3):
-        for i in range(2):
-            part_a(d, i).wait_send()
-        for e in (1, 2, 3):
-            part_b(d, e).wait_send()
+        for d in (1, 2, 3):
+            part_c(h, d).wait_send()
+
+    for d in turn:
+        part_own(d).wait_send()
+    for at, way in ((3, upwards), (0, downwards)):
+
+        @pl.when(zl == at)
+        def _(way=way):
+            for h in range(4):
+                for copy in parts_z(h, way):
+                    copy.wait_send()
 
     @pl.when(jnp.logical_not(last))
     def _():
@@ -383,13 +381,14 @@
             pltpu.VMEM((8, 2, BLK, HD), BF),
             pltpu.VMEM((4, 256, 512), BF),
             pltpu.VMEM((8, 2, BLK, HD), BF),
+            pltpu.VMEM((2, 256, HD), F32),
             dma((4, 4)), dma((4,)), dma((1,)),
-            dma((4, 2)), dma((4, 2)), dma((4, 4)), dma((4, 4)), dma((4, 2)), dma((4, 2)), dma((4, 2)), dma((4, 2)),
+            dma((4,)), dma((4,)), dma((4, 6)), dma((4, 4)), dma((4, 4)), dma((4, 4)),
             dma((4, 4)), dma((4, 4)), dma((4, 2, 2)), dma((4, 2, 2)), dma((4,)), dma((4,)), dma((4,)),
             dma((4,)), dma((4,)), dma((4, 2)), dma((8,)), dma((8, 2)),
         ],
         compiler_params=pltpu.CompilerParams(
-            collective_id=0, has_side_effects=True, vmem_limit_bytes=48 << 20
+            collective_id=0, has_side_effects=True, vmem_limit_bytes=60 << 20
         ),
         cost_estimate=pl.CostEstimate(flops=4 << 30, bytes_accessed=8 << 20, transcendentals=4 << 20),
         name="tree_attention_backward",

time: 72.1 us -> 53.4 us (0.74)
  the two profiles are of different devices: /device:TPU:69 before, /device:TPU:7 now
where the time goes in v2:
time: 53.4 us; the launch traced here: 53.2 us
  Pallas kernels  48.5 us (91%)
  local copies, waits for them, and re-layouts  4.08 us (8%)
  between operations  0.65 us (1%)
    pallas_call x1, Pallas kernels, shards(): pl.pallas_call(kernel, out_shape=[jax.ShapeDtypeStruct(queries.shape, BF)...  48.5 us
    unnamed x7, local copies, waits for them, and re-layouts  4.08 us

profile of v2, /device:TPU:7, one launch (start us, length us, event | category | flops | bytes accessed | tf_op | source)
XLA Modules:
  0.0 53.2 jit_solution(6777399145850090858)
XLA Ops:
  0.6 48.5 %tree_attention_backward.1 = (bf16[128,4096]{1,0:T(8,128)(2,1)}, bf16[128,1024]{1,0:T(8,128)(2,1)}, bf16[128,1024]{1,0:T(8,128)(2,1)}) custom-call(bf16[128,4096]{1,0:T(8,128)(2,1)} %q_hbm.1, bf16[128,4096]{1,0:T(8,128)(2,1)} %u_hbm.1, bf16[128,1024]{1,0:T(8,128)(2,1)} %k_hbm.1, bf16[128,1024]{1,0:T(8,128)(2,1)} %v_hbm.1, bf16[8,32,128]{2,1,0:T(8,128)(2,1)} %pk_hbm.1, ...), custom_call_target="tpu_custom_call" | custom-call | flops 4294967296 | bytes 8388608 | tf_op jit(solution)/shard_map/tree_attention_backward/pallas_call | solution.py:361
  49.1 0.0 copy-start.1
  49.1 2.3 %copy.14 = bf16[128,4096]{1,0:T(8,128)(2,1)} copy(bf16[128,4096]{1,0:T(8,128)(2,1)} %get-tuple-element.6) | data formatting | bytes 2097152
  51.4 0.0 copy-done.1
  51.4 0.0 copy-start
  51.4 0.7 %copy.15 = bf16[128,1024]{1,0:T(8,128)(2,1)} copy(bf16[128,1024]{1,0:T(8,128)(2,1)S(1)} %copy-done.1) | data formatting | bytes 524288
  52.1 0.3 copy-done
  52.5 0.7 %copy.16 = bf16[128,1024]{1,0:T(8,128)(2,1)} copy(bf16[128,1024]{1,0:T(8,128)(2,1)S(1)} %copy-done) | data formatting | bytes 524288
Async XLA Ops:
  49.1 2.3 %copy-start.1 = (bf16[128,1024]{1,0:T(8,128)(2,1)S(1)}, bf16[128,1024]{1,0:T(8,128)(2,1)}, u32[]{:S(2)}) copy-start(bf16[128,1024]{1,0:T(8,128)(2,1)} %get-tuple-element.7) | copy-start | bytes 786436
  51.4 1.0 %copy-start = (bf16[128,1024]{1,0:T(8,128)(2,1)S(1)}, bf16[128,1024]{1,0:T(8,128)(2,1)}, u32[]{:S(2)}) copy-start(bf16[128,1024]{1,0:T(8,128)(2,1)} %get-tuple-element.8) | copy-start | bytes 786436

commit v3 on v2

--- a/solution.py
+++ b/solution.py
@@ -25,29 +25,74 @@
     return lax.dot_general(a, b, dims, preferred_element_type=F32)
 
 
-def tile_grads(q, u, pk, pv, kw, vw, bias, pk_t, kw_t):
-    bias = jnp.concatenate([bias] * 4, 1)
-    sp = dot(pk, q, NT) * SCALE2
-    sw = dot(kw, q, NT) * SCALE2 + bias
-    peak = jnp.maximum(jnp.max(sp, 0, keepdims=True), jnp.max(sw, 0, keepdims=True))
-    ep = jnp.exp2(sp - peak)
-    ew = jnp.exp2(sw - peak)
-    inv = 1.0 / (jnp.sum(ep, 0, keepdims=True) + jnp.sum(ew, 0, keepdims=True))
-    dp = dot(pv, u, NT)
-    dw = dot(vw, u, NT)
-    center = (jnp.sum(ep * dp, 0, keepdims=True) + jnp.sum(ew * dw, 0, keepdims=True)) * inv
-    inv_s = inv * SCALE
-    dsp = ((ep * inv_s) * (dp - center)).astype(BF)
-    dsw = ((ew * inv_s) * (dw - center)).astype(BF)
-    w = (ew * inv).astype(BF)
-    gq = (dot(pk_t, dsp, NN) + dot(kw_t, dsw, NN)).T
-    return gq, dot(dsw, q, NN), dot(w, u, NN)
+def spread(rows):
+    return jnp.concatenate([rows[:, g * HD : (g + 1) * HD] for g in range(4)], 0)
+
+
+def causal_block():
+    keys = lax.broadcasted_iota(jnp.int32, (BLK, BLK), 0)
+    at = lax.broadcasted_iota(jnp.int32, (BLK, BLK), 1)
+    return keys <= at
+
+
+def window_scores(q, u, kw, vw, bias, causal):
+    def products(a, b):
+        first, middle, last = [dot(a[i * BLK : (i + 1) * BLK], b, NT) for i in range(3)]
+        return jnp.concatenate([middle, jnp.where(causal, last, first)], 0)
+
+    sw = products(kw, q) * SCALE2 + bias
+    return sw, products(vw, u), jnp.max(sw, 0, keepdims=True)
+
+
+def unfold(both, causal):
+    middle, shared = both[:BLK], both[BLK:]
+    zero = jnp.zeros_like(shared)
+    return jnp.concatenate([jnp.where(causal, zero, shared), middle, jnp.where(causal, shared, zero)], 0)
+
+
+class Tile:
+    def __init__(self, q, u, pk, pv, pk_t, kw_t, sw, dw, top):
+        self.q, self.u, self.pk, self.pv, self.pk_t, self.kw_t = q, u, pk, pv, pk_t, kw_t
+        self.sw, self.dw, self.peak = sw, dw, top
+        self.sp, self.dp, self.ep, self.ds = [], [], [], []
+
+    def scores(self, j):
+        part = slice(j * BLK, (j + 1) * BLK)
+        self.sp.append(dot(self.pk[part], self.q, NT))
+        self.dp.append(dot(self.pv[part], self.u, NT))
+        self.peak = jnp.maximum(self.peak, jnp.max(self.sp[j], 0, keepdims=True) * SCALE2)
+
+    def begin(self):
+        self.ew = jnp.exp2(self.sw[...] - self.peak)
+        self.total = jnp.sum(self.ew, 0, keepdims=True)
+        self.center = jnp.sum(self.ew * self.dw[...], 0, keepdims=True)
+
+    def expo(self, j):
+        e = jnp.exp2(self.sp[j] * SCALE2 - self.peak)
+        self.ep.append(e)
+        self.total = self.total + jnp.sum(e, 0, keepdims=True)
+        self.center = self.center + jnp.sum(e * self.dp[j], 0, keepdims=True)
+
+    def window(self, causal):
+        self.inv = 1.0 / self.total
+        self.center = self.center * self.inv
+        w = self.ew * self.inv
+        dsw = ((w * SCALE) * (self.dw[...] - self.center)).astype(BF)
+        self.dsw = unfold(dsw, causal)
+        return dot(self.dsw, self.q, NN), dot(unfold(w.astype(BF), causal), self.u, NN)
+
+    def dscores(self, j):
+        self.ds.append(((self.ep[j] * (self.inv * SCALE)) * (self.dp[j] - self.center)).astype(BF))
+
+    def grad_queries(self):
+        keys = jnp.concatenate([self.pk_t, self.kw_t], 1)
+        return dot(keys, jnp.concatenate(self.ds + [self.dsw], 0), NN).astype(BF).T
 
 
 def kernel(
     q_hbm, u_hbm, k_hbm, v_hbm, pk_hbm, pv_hbm, ids_hbm, pat_hbm,
     gq_hbm, gk_hbm, gv_hbm,
-    ids, pat, bias, qb, ub, kw, vw, pkv, gs, gown, gnext, gqb, fin, acc,
+    ids, pat, bias, qb, ub, kw, vw, pkv, gs, gown, gnext, gqb, fin, sbuf, dbuf, top,
     sem_in, sem_small, sem_own,
     snd_own, rcv_own, snd_z, rcv_z, snd_c, rcv_c,
     snd_sib, rcv_sib, snd_halo, rcv_halo, snd_gq, rcv_gq, sem_gq,
@@ -86,9 +131,9 @@
     def greet(where):
         pl.semaphore_signal(barrier, inc=1, device_id=where, device_id_type=MESH)
 
-    upwards = [(2, 2, 1), (2, 2, 0), (3, 1, 3), (3, 1, 2), (3, 1, 1), (3, 1, 0)]
-    downwards = [(2, 2, 2), (2, 2, 3), (1, 3, 0), (1, 3, 1), (1, 3, 2), (1, 3, 3)]
-    source = {1: along_z(1, 0), 2: along_z(2, jnp.where(zl < 2, 3, 0)), 3: along_z(3, 3)}
+    upwards = [(3, 2, 1), (3, 2, 0), (2, 1, 3), (2, 1, 2), (2, 1, 1), (2, 1, 0)]
+    downwards = [(3, 2, 2), (3, 2, 3), (1, 3, 0), (1, 3, 1), (1, 3, 2), (1, 3, 3)]
+    source = {1: along_z(1, 0), 2: along_z(3, 3), 3: along_z(2, jnp.where(zl < 2, 3, 0))}
     for where in [sib] + y_peer[1:] + list(source.values()):
         greet(where)
 
@@ -139,9 +184,10 @@
     def parts_z(h, way):
         return [part_z(h, j, slot, along_z(d, to_zl)) for j, (slot, d, to_zl) in enumerate(way)]
 
-    def part_c(h, d):
-        src, dst = pkv.at[h, :, 0, 1:4], pkv.at[h, :, 4 - d, 1:4]
-        return send(src, dst, snd_c.at[h, d], rcv_c.at[h, d], y_peer[d])
+    def part_c(h, d, far):
+        sub = slice(3, 4) if far else slice(1, 3)
+        src, dst = pkv.at[h, :, 0, sub], pkv.at[h, :, 4 - d, sub]
+        return send(src, dst, snd_c.at[far, h, d], rcv_c.at[far, h, d], y_peer[d])
 
     turn = (2, 1, 3)
 
@@ -202,60 +248,44 @@
     ] + [ids[:, pl.ds(pl.multiple_of(c * 256 + b * BLK, BLK), BLK)].astype(F32) for b in range(2)]
     wide = [jnp.broadcast_to(r, (BLK, BLK)) for r in id_rows]
     tall = [w.T for w in wide]
-    key_at = lax.broadcasted_iota(jnp.int32, (BLK, BLK), 0)
-    row_at = lax.broadcasted_iota(jnp.int32, (BLK, BLK), 1)
+    causal1 = causal_block()
+    causal = jnp.concatenate([causal1] * 4, 1)
     inside = jnp.where(first, 0, 1)
     for rb in range(2):
         at = 2 * c + rb
-        for t in range(3):
-            b = rb + t
-            seen = tall[b] == wide[2 + rb]
-            if t == 2:
-                seen = seen & (key_at <= row_at)
-            else:
-                flag = pat[0, at, jnp.maximum(at - 2 + t, 0)]
-                if b < 2:
-                    flag = flag * inside
-                seen = seen & (jnp.full((BLK, BLK), flag, jnp.int32) > 0)
-            bias[rb, t * BLK : (t + 1) * BLK] = jnp.where(seen, 0.0, HIDE)
-
-    def along_y(h):
-        for slot in (1, 3, 2):
+
+        def earlier(step, rb=rb, at=at):
+            b = rb + 2 - step
+            flag = pat[0, at, jnp.maximum(at - step, 0)]
+            if b < 2:
+                flag = flag * inside
+            return (tall[b] == wide[2 + rb]) & (jnp.full((BLK, BLK), flag, jnp.int32) > 0)
+
+        own = tall[2 + rb] == wide[2 + rb]
+        shared = (causal1 & own) | (jnp.logical_not(causal1) & earlier(2))
+        for i, seen in enumerate((earlier(1), shared)):
+            part = jnp.where(seen, 0.0, HIDE)
+            bias[rb, i * BLK : (i + 1) * BLK] = jnp.concatenate([part] * 4, 1)
+
+    def along_y(h, between=None):
+        for slot in (1, 2):
             part_z(h, 0, slot, source[slot]).wait_recv()
         for d in turn:
-            part_c(h, d).start()
-
-    along_y(0)
-    pl.when((x == 3) & jnp.logical_not(last))(halos)
-    along_y(1)
-    for d in turn:
-        part_own(d).wait_recv()
-
-    def to_prev(h, core):
-        part = gs.at[h, :, core * BLK : (core + 1) * BLK]
-        return send(part, gnext.at[k * 4 + h], snd_gprev.at[h, core], rcv_gnext.at[k * 4 + h], prv[core])
-
-    def grads_to_sib(h):
-        return send(gs.at[h, :, sib_rows], gown.at[k * 4 + h], snd_gsib.at[h], rcv_gsib.at[h], sib)
-
-    def gq_own(h):
-        return pltpu.make_async_copy(gqb.at[h, rows], gq_hbm.at[:, cols(k, h, 512)], sem_gq.at[h])
-
-    def gq_to_sib(h):
-        return send(gqb.at[h, other], gq_hbm.at[:, cols(k, h, 512)], snd_gq.at[h], rcv_gq.at[h], sib)
-
-    @pl.loop(0, 4)
-    def _(h):
-        @pl.when(h < 2)
-        def _():
-            along_y(h + 2)
-
+            part_c(h, d, 0).start()
+        if between is not None:
+            between()
+        part_z(h, 0, 3, source[3]).wait_recv()
+        for d in turn:
+            part_c(h, d, 1).start()
+
+    def late_halos(h):
+        pl.when((h == 0) & (x == 3) & jnp.logical_not(last))(halos)
+
+    def window_part(h):
         for copy in own_parts(h):
             copy.wait()
         for copy in to_sib(h):
             copy.wait_recv()
-        for d in turn:
-            part_c(h, d).wait_recv()
 
         @pl.when(jnp.logical_not(first))
         def _():
@@ -264,32 +294,93 @@
                     dst = (kw, vw)[i].at[h, core * BLK : (core + 1) * BLK]
                     send(dst, dst, snd_halo.at[h, core, i], rcv_halo.at[h, core, i], prv[0]).wait_recv()
 
+        for rb in range(2):
+            q = spread(qb[h, rb * BLK : (rb + 1) * BLK])
+            u = spread(ub[h, rb * BLK : (rb + 1) * BLK])
+            near = slice(rb * BLK, rb * BLK + 384)
+            sbuf[h, rb], dbuf[h, rb], top[h, rb] = window_scores(q, u, kw[h, near], vw[h, near], bias[rb], causal)
+
+    early = (x > 0) | first
+
+    @pl.loop(0, 4)
+    def _(h):
+        pl.when(early)(lambda: window_part(h))
+
+        @pl.when(h < 3)
+        def _():
+            along_y(h, lambda: late_halos(h))
+
+    for d in turn:
+        part_own(d).wait_recv()
+
+    def to_prev(h, core):
+        part = gs.at[h, :, core * BLK : (core + 1) * BLK]
+        return send(part, gnext.at[k * 4 + h], snd_gprev.at[h, core], rcv_gnext.at[k * 4 + h], prv[core])
+
+    def grads_to_sib(h):
+        return send(gs.at[h, :, sib_rows], gown.at[k * 4 + h], snd_gsib.at[h], rcv_gsib.at[h], sib)
+
+    def gq_own(h):
+        return pltpu.make_async_copy(gqb.at[h, rows], gq_hbm.at[:, cols(k, h, 512)], sem_gq.at[h])
+
+    def gq_to_sib(h):
+        return send(gqb.at[h, other], gq_hbm.at[:, cols(k, h, 512)], snd_gq.at[h], rcv_gq.at[h], sib)
+
+    @pl.loop(0, 4)
+    def _(h):
+        @pl.when(h == 1)
+        def _():
+            along_y(3)
+
+        pl.when(jnp.logical_not(early))(lambda: window_part(h))
+        for d in turn:
+            for far in range(2):
+                part_c(h, d, far).wait_recv()
+
         pk = pkv[h, 0].reshape(512, HD)
         pv = pkv[h, 1].reshape(512, HD)
         pk_t = pk.T
         kw_t = kw[h].T
 
-        def half(rb):
-            qr = qb[h, rb * BLK : (rb + 1) * BLK]
-            ur = ub[h, rb * BLK : (rb + 1) * BLK]
-            q = jnp.concatenate([qr[:, g * HD : (g + 1) * HD] for g in range(4)], 0)
-            u = jnp.concatenate([ur[:, g * HD : (g + 1) * HD] for g in range(4)], 0)
-            near = slice(rb * BLK, rb * BLK + 384)
-            gq, gk, gv = tile_grads(q, u, pk, pv, kw[h, near], vw[h, near], bias[rb], pk_t, kw_t[:, near])
+        a, b = [
+            Tile(
+                spread(qb[h, rb * BLK : (rb + 1) * BLK]),
+                spread(ub[h, rb * BLK : (rb + 1) * BLK]),
+                pk, pv, pk_t, kw_t[:, rb * BLK : rb * BLK + 384],
+                sbuf.at[h, rb], dbuf.at[h, rb], top[h, rb],
+            )
+            for rb in range(2)
+        ]
+
+        def store_gq(rb, gq):
             for g in range(4):
-                gqb[h, rb * BLK : (rb + 1) * BLK, g * HD : (g + 1) * HD] = gq[g * BLK : (g + 1) * BLK].astype(BF)
-            return gk, gv
-
-        a = half(0)
+                gqb[h, rb * BLK : (rb + 1) * BLK, g * HD : (g + 1) * HD] = gq[g * BLK : (g + 1) * BLK]
+
+        for j in range(4):
+            a.scores(j)
+        a.begin()
+        for j in range(4):
+            b.scores(j)
+            a.expo(j)
+        grads_a = a.window(causal)
+        b.begin()
+        for j in range(4):
+            b.expo(j)
+        grads_b = b.window(causal)
         for i in range(2):
-            gs[h, i, 0:128] = a[i][0:128].astype(BF)
-            acc[i] = a[i][128:384]
-        pl.when(jnp.logical_not(first))(to_prev(h, 0).start)
-        b = half(1)
-        for i in range(2):
-            gs[h, i, 128:384] = (acc[i] + b[i][0:256]).astype(BF)
-            gs[h, i, 384:512] = b[i][256:384].astype(BF)
-        pl.when(jnp.logical_not(first))(to_prev(h, 1).start)
+            gs[h, i, 0:128] = grads_a[i][0:128].astype(BF)
+            gs[h, i, 128:384] = (grads_a[i][128:384] + grads_b[i][0:256]).astype(BF)
+            gs[h, i, 384:512] = grads_b[i][256:384].astype(BF)
+
+        @pl.when(jnp.logical_not(first))
+        def _():
+            to_prev(h, 0).start()
+            to_prev(h, 1).start()
+
+        for rb, tile in enumerate((a, b)):
+            for j in range(4):
+                tile.dscores(j)
+            store_gq(rb, tile.grad_queries())
 
         grads_to_sib(h).start()
         gq_to_sib(h).start()
@@ -325,7 +416,8 @@
         for copy in to_sib(h):
             copy.wait_send()
         for d in (1, 2, 3):
-            part_c(h, d).wait_send()
+            for far in range(2):
+                part_c(h, d, far).wait_send()
 
     for d in turn:
         part_own(d).wait_send()
@@ -355,22 +447,35 @@
             copy.wait()
 
 
+def hand_over(gq, gk, gv, gq_out, gk_out, gv_out, gq_at, gk_at, gv_at, sem_in, sem_out):
+    parts = [(ref, slice(0, BLK)) for ref in ((gk, gk_at, gk_out), (gv, gv_at, gv_out))]
+    parts += [((gq, gq_at, gq_out), slice(i * 32, (i + 1) * 32)) for i in range(4)]
+    loads, stores = [], []
+    for i, ((src, at, out), part) in enumerate(parts):
+        loads.append(pltpu.make_async_copy(src.at[part], at.at[part], sem_in.at[i]))
+        stores.append(pltpu.make_async_copy(at.at[part], out.at[part], sem_out.at[i]))
+    for copy in loads:
+        copy.start()
+    for load, store in zip(loads, stores):
+        load.wait()
+        store.start()
+    for copy in stores:
+        copy.wait()
+
+
 def shards(queries, keys, values, cotangent, prompt_keys, prompt_values, response_ids, block_pattern):
     anywhere = pl.BlockSpec(memory_space=pl.ANY)
     dma = pltpu.SemaphoreType.DMA
-    return pl.pallas_call(
+    shapes = [jax.ShapeDtypeStruct(a.shape, BF) for a in (queries, keys, values)]
+    grads = pl.pallas_call(
         kernel,
-        out_shape=[
-            jax.ShapeDtypeStruct(queries.shape, BF),
-            jax.ShapeDtypeStruct(keys.shape, BF),
-            jax.ShapeDtypeStruct(values.shape, BF),
-        ],
+        out_shape=shapes,
         in_specs=[anywhere] * 8,
         out_specs=[anywhere] * 3,
         scratch_shapes=[
             pltpu.VMEM((1, 4096), jnp.int32),
             pltpu.SMEM((1, 32, 32), jnp.int32),
-            pltpu.VMEM((2, 384, BLK), F32),
+            pltpu.VMEM((2, 256, 512), F32),
             pltpu.VMEM((4, 256, 512), BF),
             pltpu.VMEM((4, 256, 512), BF),
             pltpu.VMEM((4, 512, HD), BF),
@@ -381,9 +486,11 @@
             pltpu.VMEM((8, 2, BLK, HD), BF),
             pltpu.VMEM((4, 256, 512), BF),
             pltpu.VMEM((8, 2, BLK, HD), BF),
-            pltpu.VMEM((2, 256, HD), F32),
+            pltpu.VMEM((4, 2, 256, 512), F32),
+            pltpu.VMEM((4, 2, 256, 512), F32),
+            pltpu.VMEM((4, 2, 1, 512), F32),
             dma((4, 4)), dma((4,)), dma((1,)),
-            dma((4,)), dma((4,)), dma((4, 6)), dma((4, 4)), dma((4, 4)), dma((4, 4)),
+            dma((4,)), dma((4,)), dma((4, 6)), dma((4, 4)), dma((2, 4, 4)), dma((2, 4, 4)),
             dma((4, 4)), dma((4, 4)), dma((4, 2, 2)), dma((4, 2, 2)), dma((4,)), dma((4,)), dma((4,)),
             dma((4,)), dma((4,)), dma((4, 2)), dma((8,)), dma((8, 2)),
         ],
@@ -393,6 +500,15 @@
         cost_estimate=pl.CostEstimate(flops=4 << 30, bytes_accessed=8 << 20, transcendentals=4 << 20),
         name="tree_attention_backward",
     )(queries, cotangent, keys, values, prompt_keys, prompt_values, response_ids, block_pattern)
+    return pl.pallas_call(
+        hand_over,
+        out_shape=shapes,
+        in_specs=[anywhere] * 3,
+        out_specs=[anywhere] * 3,
+        scratch_shapes=[pltpu.VMEM(a.shape, BF) for a in shapes] + [dma((6,)), dma((6,))],
+        compiler_params=pltpu.CompilerParams(vmem_limit_bytes=60 << 20),
+        name="hand_over",
+    )(*grads)
 
 
 def solution(mesh):

time: 53.4 us -> 51.5 us (0.964)
  local copies, waits for them, and re-layouts: 4.08 us -> 0 us
  Pallas kernels: 48.5 us -> 50.7 us
    unnamed x7 -> x0, local copies, waits for them, and re-layouts: 4.08 us -> none
    pallas_call x1 -> x2, Pallas kernels: 48.5 us -> 50.7 us  [the longest x1 48.5 us: shards(): pl.pallas_call(kernel, out_shape=shapes, in_specs=[anywhere] * 8, out_spe...]
where the time goes in v3:
time: 51.5 us; the launch traced here: 51.3 us
  Pallas kernels  50.7 us (98%)
  between operations  0.64 us (1%)
    pallas_call x1, Pallas kernels, shards(): pl.pallas_call(kernel, out_shape=shapes, in_specs=[anywhere] * 8, out_spe...  48.5 us
    pallas_call x1, Pallas kernels, shards(): pl.pallas_call(hand_over, out_shape=shapes, in_specs=[anywhere] * 3, out_...  2.19 us

profile of v3, /device:TPU:7, one launch (start us, length us, event | category | flops | bytes accessed | tf_op | source)
XLA Modules:
  0.0 51.3 jit_solution(4403156632071223039)
XLA Ops:
  0.6 48.5 %tree_attention_backward.1 = (bf16[128,4096]{1,0:T(8,128)(2,1)}, bf16[128,1024]{1,0:T(8,128)(2,1)}, bf16[128,1024]{1,0:T(8,128)(2,1)}) custom-call(bf16[128,4096]{1,0:T(8,128)(2,1)} %q_hbm.1, bf16[128,4096]{1,0:T(8,128)(2,1)} %u_hbm.1, bf16[128,1024]{1,0:T(8,128)(2,1)} %k_hbm.1, bf16[128,1024]{1,0:T(8,128)(2,1)} %v_hbm.1, bf16[8,32,128]{2,1,0:T(8,128)(2,1)} %pk_hbm.1, ...), custom_call_target="tpu_custom_call" | custom-call | flops 4294967296 | bytes 8388608 | tf_op jit(solution)/shard_map/tree_attention_backward/pallas_call | solution.py:470
  49.1 2.2 %hand_over.1 = (bf16[128,4096]{1,0:T(8,128)(2,1)}, bf16[128,1024]{1,0:T(8,128)(2,1)}, bf16[128,1024]{1,0:T(8,128)(2,1)}) custom-call(bf16[128,4096]{1,0:T(8,128)(2,1)} %get-tuple-element.6.gq, bf16[128,1024]{1,0:T(8,128)(2,1)} %get-tuple-element.7.gk, bf16[128,1024]{1,0:T(8,128)(2,1)} %get-tuple-element.8.gv), custom_call_target="tpu_custom_call" | custom-call | tf_op jit(solution)/shard_map/hand_over/pallas_call | solution.py:503

commit v4 on v3

--- a/solution.py
+++ b/solution.py
@@ -37,8 +37,8 @@
 
 def window_scores(q, u, kw, vw, bias, causal):
     def products(a, b):
-        first, middle, last = [dot(a[i * BLK : (i + 1) * BLK], b, NT) for i in range(3)]
-        return jnp.concatenate([middle, jnp.where(causal, last, first)], 0)
+        out = dot(a, b, NT)
+        return jnp.concatenate([out[BLK : 2 * BLK], jnp.where(causal, out[2 * BLK :], out[:BLK])], 0)
 
     sw = products(kw, q) * SCALE2 + bias
     return sw, products(vw, u), jnp.max(sw, 0, keepdims=True)
@@ -54,39 +54,32 @@
     def __init__(self, q, u, pk, pv, pk_t, kw_t, sw, dw, top):
         self.q, self.u, self.pk, self.pv, self.pk_t, self.kw_t = q, u, pk, pv, pk_t, kw_t
         self.sw, self.dw, self.peak = sw, dw, top
-        self.sp, self.dp, self.ep, self.ds = [], [], [], []
-
-    def scores(self, j):
-        part = slice(j * BLK, (j + 1) * BLK)
-        self.sp.append(dot(self.pk[part], self.q, NT))
-        self.dp.append(dot(self.pv[part], self.u, NT))
-        self.peak = jnp.maximum(self.peak, jnp.max(self.sp[j], 0, keepdims=True) * SCALE2)
-
-    def begin(self):
+
+    def scores(self):
+        self.sp = dot(self.pk, self.q, NT)
+        self.peak = jnp.maximum(self.peak, jnp.max(self.sp, 0, keepdims=True) * SCALE2)
+        self.dp = dot(self.pv, self.u, NT)
+
+    def expo(self):
         self.ew = jnp.exp2(self.sw[...] - self.peak)
-        self.total = jnp.sum(self.ew, 0, keepdims=True)
-        self.center = jnp.sum(self.ew * self.dw[...], 0, keepdims=True)
-
-    def expo(self, j):
-        e = jnp.exp2(self.sp[j] * SCALE2 - self.peak)
-        self.ep.append(e)
-        self.total = self.total + jnp.sum(e, 0, keepdims=True)
-        self.center = self.center + jnp.sum(e * self.dp[j], 0, keepdims=True)
+        self.ep = jnp.exp2(self.sp * SCALE2 - self.peak)
+        total = jnp.sum(self.ew, 0, keepdims=True) + jnp.sum(self.ep, 0, keepdims=True)
+        center = jnp.sum(self.ew * self.dw[...], 0, keepdims=True) + jnp.sum(self.ep * self.dp, 0, keepdims=True)
+        self.inv = 1.0 / total
+        self.center = center * self.inv
 
     def window(self, causal):
-        self.inv = 1.0 / self.total
-        self.center = self.center * self.inv
         w = self.ew * self.inv
         dsw = ((w * SCALE) * (self.dw[...] - self.center)).astype(BF)
         self.dsw = unfold(dsw, causal)
         return dot(self.dsw, self.q, NN), dot(unfold(w.astype(BF), causal), self.u, NN)
 
-    def dscores(self, j):
-        self.ds.append(((self.ep[j] * (self.inv * SCALE)) * (self.dp[j] - self.center)).astype(BF))
+    def dscores(self):
+        self.ds = (self.ep * (self.dp - self.center)).astype(BF)
 
     def grad_queries(self):
-        keys = jnp.concatenate([self.pk_t, self.kw_t], 1)
-        return dot(keys, jnp.concatenate(self.ds + [self.dsw], 0), NN).astype(BF).T
+        prompt = dot(self.pk_t, self.ds, NN) * (self.inv * SCALE)
+        return (prompt + dot(self.kw_t, self.dsw, NN)).astype(BF).T
 
 
 def kernel(
@@ -356,17 +349,11 @@
             for g in range(4):
                 gqb[h, rb * BLK : (rb + 1) * BLK, g * HD : (g + 1) * HD] = gq[g * BLK : (g + 1) * BLK]
 
-        for j in range(4):
-            a.scores(j)
-        a.begin()
-        for j in range(4):
-            b.scores(j)
-            a.expo(j)
-        grads_a = a.window(causal)
-        b.begin()
-        for j in range(4):
-            b.expo(j)
-        grads_b = b.window(causal)
+        for tile in (a, b):
+            tile.scores()
+        for tile in (a, b):
+            tile.expo()
+        grads_a, grads_b = a.window(causal), b.window(causal)
         for i in range(2):
             gs[h, i, 0:128] = grads_a[i][0:128].astype(BF)
             gs[h, i, 128:384] = (grads_a[i][128:384] + grads_b[i][0:256]).astype(BF)
@@ -377,9 +364,9 @@
             to_prev(h, 0).start()
             to_prev(h, 1).start()
 
+        for tile in (a, b):
+            tile.dscores()
         for rb, tile in enumerate((a, b)):
-            for j in range(4):
-                tile.dscores(j)
             store_gq(rb, tile.grad_queries())
 
         grads_to_sib(h).start()

time: 51.5 us -> 50 us (0.971)
  Pallas kernels: 50.7 us -> 49.2 us
    pallas_call x1, Pallas kernels: 48.5 us -> 47.1 us  [shards(): pl.pallas_call(kernel, out_shape=shapes, in_specs=[anywhere] * 8, out_spe...]
where the time goes in v4:
time: 50 us; the launch traced here: 49.9 us
  Pallas kernels  49.2 us (98%)
  between operations  0.64 us (1%)
    pallas_call x1, Pallas kernels, shards(): pl.pallas_call(kernel, out_shape=shapes, in_specs=[anywhere] * 8, out_spe...  47.1 us
    pallas_call x1, Pallas kernels, shards(): pl.pallas_call(hand_over, out_shape=shapes, in_specs=[anywhere] * 3, out_...  2.19 us

profile of v4, /device:TPU:7, one launch (start us, length us, event | category | flops | bytes accessed | tf_op | source)
XLA Modules:
  0.0 49.9 jit_solution(9369696693766679320)
XLA Ops:
  0.6 47.1 %tree_attention_backward.1 = (bf16[128,4096]{1,0:T(8,128)(2,1)}, bf16[128,1024]{1,0:T(8,128)(2,1)}, bf16[128,1024]{1,0:T(8,128)(2,1)}) custom-call(bf16[128,4096]{1,0:T(8,128)(2,1)} %q_hbm.1, bf16[128,4096]{1,0:T(8,128)(2,1)} %u_hbm.1, bf16[128,1024]{1,0:T(8,128)(2,1)} %k_hbm.1, bf16[128,1024]{1,0:T(8,128)(2,1)} %v_hbm.1, bf16[8,32,128]{2,1,0:T(8,128)(2,1)} %pk_hbm.1, ...), custom_call_target="tpu_custom_call" | custom-call | flops 4294967296 | bytes 8388608 | tf_op jit(solution)/shard_map/tree_attention_backward/pallas_call | solution.py:457
  47.7 2.2 %hand_over.1 = (bf16[128,4096]{1,0:T(8,128)(2,1)}, bf16[128,1024]{1,0:T(8,128)(2,1)}, bf16[128,1024]{1,0:T(8,128)(2,1)}) custom-call(bf16[128,4096]{1,0:T(8,128)(2,1)} %get-tuple-element.6.gq, bf16[128,1024]{1,0:T(8,128)(2,1)} %get-tuple-element.7.gk, bf16[128,1024]{1,0:T(8,128)(2,1)} %get-tuple-element.8.gv), custom_call_target="tpu_custom_call" | custom-call | tf_op jit(solution)/shard_map/hand_over/pallas_call | solution.py:490

commit v5 on v4

--- a/solution.py
+++ b/solution.py
@@ -84,12 +84,12 @@
 
 def kernel(
     q_hbm, u_hbm, k_hbm, v_hbm, pk_hbm, pv_hbm, ids_hbm, pat_hbm,
-    gq_hbm, gk_hbm, gv_hbm,
-    ids, pat, bias, qb, ub, kw, vw, pkv, gs, gown, gnext, gqb, fin, sbuf, dbuf, top,
+    gq_hbm, gown, gnext,
+    ids, pat, bias, qb, ub, kw, vw, pkv, gs, gqb, sbuf, dbuf, top,
     sem_in, sem_small, sem_own,
     snd_own, rcv_own, snd_z, rcv_z, snd_c, rcv_c,
     snd_sib, rcv_sib, snd_halo, rcv_halo, snd_gq, rcv_gq, sem_gq,
-    snd_gsib, rcv_gsib, snd_gprev, rcv_gnext, sem_out,
+    snd_gsib, rcv_gsib, snd_gprev, rcv_gnext, sem_gown,
 ):
     s = lax.axis_index("sample")
     hd = lax.axis_index("head")
@@ -228,10 +228,6 @@
     def _():
         kw[:, 0:256] = jnp.zeros((4, 256, HD), BF)
         vw[:, 0:256] = jnp.zeros((4, 256, HD), BF)
-
-    @pl.when(last)
-    def _():
-        gnext[...] = jnp.zeros((8, 2, BLK, HD), BF)
 
     for copy in small:
         copy.wait()
@@ -313,6 +309,9 @@
     def grads_to_sib(h):
         return send(gs.at[h, :, sib_rows], gown.at[k * 4 + h], snd_gsib.at[h], rcv_gsib.at[h], sib)
 
+    def keep(h):
+        return pltpu.make_async_copy(gs.at[h, :, own_rows], gown.at[k * 4 + h], sem_gown.at[h])
+
     def gq_own(h):
         return pltpu.make_async_copy(gqb.at[h, rows], gq_hbm.at[:, cols(k, h, 512)], sem_gq.at[h])
 
@@ -372,13 +371,7 @@
         grads_to_sib(h).start()
         gq_to_sib(h).start()
         gq_own(h).start()
-        gown[k * 4 + h] = gs[h, :, own_rows]
-
-    def outs(hh):
-        return [
-            pltpu.make_async_copy(fin.at[hh, i], out.at[:, hh * HD : (hh + 1) * HD], sem_out.at[hh, i])
-            for i, out in enumerate((gk_hbm, gv_hbm))
-        ]
+        keep(h).start()
 
     for h in range(4):
         send(gs.at[h, :, sib_rows], gown.at[(1 - k) * 4 + h], snd_gsib.at[h], rcv_gsib.at[h], sib).wait_recv()
@@ -389,13 +382,9 @@
                 part = gnext.at[core * 4 + h]
                 send(part, part, snd_gprev.at[h, core], rcv_gnext.at[core * 4 + h], nxt[0]).wait_recv()
 
-            hh = core * 4 + h
-            fin[hh] = (gown[hh].astype(F32) + gnext[hh].astype(F32)).astype(BF)
-            for copy in outs(hh):
-                copy.start()
-
     for h in range(4):
         gq_own(h).wait()
+        keep(h).wait()
         copy = gq_to_sib(h)
         copy.wait_send()
         send(gqb.at[h, rows], gq_hbm.at[:, cols(1 - k, h, 512)], snd_gq.at[h], rcv_gq.at[h], sib).wait_recv()
@@ -429,21 +418,24 @@
             for core in range(2):
                 to_prev(h, core).wait_send()
 
-    for hh in range(KVH):
-        for copy in outs(hh):
-            copy.wait()
-
-
-def hand_over(gq, gk, gv, gq_out, gk_out, gv_out, gq_at, gk_at, gv_at, sem_in, sem_out):
-    parts = [(ref, slice(0, BLK)) for ref in ((gk, gk_at, gk_out), (gv, gv_at, gv_out))]
-    parts += [((gq, gq_at, gq_out), slice(i * 32, (i + 1) * 32)) for i in range(4)]
-    loads, stores = [], []
-    for i, ((src, at, out), part) in enumerate(parts):
-        loads.append(pltpu.make_async_copy(src.at[part], at.at[part], sem_in.at[i]))
-        stores.append(pltpu.make_async_copy(at.at[part], out.at[part], sem_out.at[i]))
+
+def hand_over(gq, own, nxt, gq_out, gk_out, gv_out, gq_at, gk_at, gv_at, own_at, nxt_at, sem_in, sem_out):
+    quarters = [slice(i * 32, (i + 1) * 32) for i in range(4)]
+    loads = [pltpu.make_async_copy(own, own_at, sem_in.at[4]), pltpu.make_async_copy(nxt, nxt_at, sem_in.at[5])]
+    moves = [pltpu.make_async_copy(gq.at[p], gq_at.at[p], sem_in.at[i]) for i, p in enumerate(quarters)]
+    stores = [pltpu.make_async_copy(gq_at.at[p], gq_out.at[p], sem_out.at[i]) for i, p in enumerate(quarters)]
+    for copy in loads + moves:
+        copy.start()
     for copy in loads:
-        copy.start()
-    for load, store in zip(loads, stores):
+        copy.wait()
+    more = jnp.full((BLK, HD), jnp.where(lax.axis_index("head") // 2 == 15, 0, 1), jnp.int32) > 0
+    for i, (at, out) in enumerate(((gk_at, gk_out), (gv_at, gv_out))):
+        for hh in range(KVH):
+            term = jnp.where(more, nxt_at[hh, i].astype(F32), 0.0)
+            at[:, hh * HD : (hh + 1) * HD] = (own_at[hh, i].astype(F32) + term).astype(BF)
+        stores.append(pltpu.make_async_copy(at, out, sem_out.at[4 + i]))
+        stores[-1].start()
+    for load, store in zip(moves, stores):
         load.wait()
         store.start()
     for copy in stores:
@@ -454,9 +446,10 @@
     anywhere = pl.BlockSpec(memory_space=pl.ANY)
     dma = pltpu.SemaphoreType.DMA
     shapes = [jax.ShapeDtypeStruct(a.shape, BF) for a in (queries, keys, values)]
+    window = jax.ShapeDtypeStruct((KVH, 2, BLK, HD), BF)
     grads = pl.pallas_call(
         kernel,
-        out_shape=shapes,
+        out_shape=[shapes[0], window, window],
         in_specs=[anywhere] * 8,
         out_specs=[anywhere] * 3,
         scratch_shapes=[
@@ -469,17 +462,14 @@
             pltpu.VMEM((4, 512, HD), BF),
             pltpu.VMEM((4, 2, 4, 4, 32, HD), BF),
             pltpu.VMEM((4, 2, 512, HD), BF),
-            pltpu.VMEM((8, 2, BLK, HD), BF),
-            pltpu.VMEM((8, 2, BLK, HD), BF),
             pltpu.VMEM((4, 256, 512), BF),
-            pltpu.VMEM((8, 2, BLK, HD), BF),
             pltpu.VMEM((4, 2, 256, 512), F32),
             pltpu.VMEM((4, 2, 256, 512), F32),
             pltpu.VMEM((4, 2, 1, 512), F32),
             dma((4, 4)), dma((4,)), dma((1,)),
             dma((4,)), dma((4,)), dma((4, 6)), dma((4, 4)), dma((2, 4, 4)), dma((2, 4, 4)),
             dma((4, 4)), dma((4, 4)), dma((4, 2, 2)), dma((4, 2, 2)), dma((4,)), dma((4,)), dma((4,)),
-            dma((4,)), dma((4,)), dma((4, 2)), dma((8,)), dma((8, 2)),
+            dma((4,)), dma((4,)), dma((4, 2)), dma((8,)), dma((4,)),
         ],
         compiler_params=pltpu.CompilerParams(
             collective_id=0, has_side_effects=True, vmem_limit_bytes=60 << 20
@@ -492,7 +482,7 @@
         out_shape=shapes,
         in_specs=[anywhere] * 3,
         out_specs=[anywhere] * 3,
-        scratch_shapes=[pltpu.VMEM(a.shape, BF) for a in shapes] + [dma((6,)), dma((6,))],
+        scratch_shapes=[pltpu.VMEM(a.shape, BF) for a in (*shapes, window, window)] + [dma((6,)), dma((6,))],
         compiler_params=pltpu.CompilerParams(vmem_limit_bytes=60 << 20),
         name="hand_over",
     )(*grads)

time: 50 us -> 49.9 us (level)
  no operation moved by 1% of the time
where the time goes in v5:
time: 49.9 us; the launch traced here: 49.8 us
  Pallas kernels  49.2 us (99%)
  between operations  0.64 us (1%)
    pallas_call x1, Pallas kernels, shards(): pl.pallas_call(kernel, out_shape=[shapes[0], window, window], in_specs=[a...  46.6 us
    pallas_call x1, Pallas kernels, shards(): pl.pallas_call(hand_over, out_shape=shapes, in_specs=[anywhere] * 3, out_...  2.54 us

profile of v5, /device:TPU:7, one launch (start us, length us, event | category | flops | bytes accessed | tf_op | source)
XLA Modules:
  0.0 49.8 jit_solution(10355718444666533452)
XLA Ops:
  0.6 46.6 %tree_attention_backward.1 = (bf16[128,4096]{1,0:T(8,128)(2,1)}, bf16[8,2,128,128]{3,2,1,0:T(8,128)(2,1)}, bf16[8,2,128,128]{3,2,1,0:T(8,128)(2,1)}) custom-call(bf16[128,4096]{1,0:T(8,128)(2,1)} %q_hbm.1, bf16[128,4096]{1,0:T(8,128)(2,1)} %u_hbm.1, bf16[128,1024]{1,0:T(8,128)(2,1)} %k_hbm.1, bf16[128,1024]{1,0:T(8,128)(2,1)} %v_hbm.1, ...), custom_call_target="tpu_custom_call" | custom-call | flops 4294967296 | bytes 8388608 | tf_op jit(solution)/shard_map/tree_attention_backward/pallas_call | solution.py:450
  47.3 2.5 %hand_over.1 = (bf16[128,4096]{1,0:T(8,128)(2,1)}, bf16[128,1024]{1,0:T(8,128)(2,1)}, bf16[128,1024]{1,0:T(8,128)(2,1)}) custom-call(bf16[128,4096]{1,0:T(8,128)(2,1)} %get-tuple-element.6.gq, bf16[8,2,128,128]{3,2,1,0:T(8,128)(2,1)} %get-tuple-element.7.own, bf16[8,2,128,128]{3,2,1,0:T(8,128)(2,1)} %get-tuple-element.8.nxt), custom_call_target="tpu_custom_call" | custom-call | tf_op jit(solution)/shard_map/hand_over/pallas_call | solution.py:480
